TPU v7x, 512 devices: a whole 4x8x8 slice. The times are simulated.
512 devices in a mesh: dp: 8 (over z), vocab: 64 (over x, y, core).
Axes of the slice: x: 4, y: 8, z: 8, core: 2. Of those that a mesh axis runs over, the one named last changes fastest.
Arguments:
- hidden_ref: bfloat16 [1280, 4096], P('dp'), may hold values from -640 to 640
- hidden_train: bfloat16 [1280, 4096], P('dp'), may hold values from -640 to 640
- head_ref: bfloat16 [64512, 4096], P('vocab', 'dp'), may hold values from -1 to 1
- head_train: bfloat16 [64512, 4096], P('vocab', 'dp'), may hold values from -1 to 1
- targets: int32 [1280], P('dp'), may hold values from 0 to 64511
- mask: int32 [1280], P('dp'), may hold values from 0 to 1, as said below
Outputs:
- excess: float32 [1280], P('dp')
- loss_value: float32 [], replicated
- hidden_grad: float32 [4096, 1280], P('vocab', 'dp')
Inputs may be any that keep to these rules, and one draw needn't show every extreme that they name: `mask`: exactly 100 ones in each aligned block of 160 tokens.
All inputs are finite; a program needn't handle non-finite values.
Results may differ from a plain program's by a relative error of at most 0.0016.
Values may be sent and summed in bfloat16 or wider, within the bound.
A program may use at most 64 MiB of HBM per device.

v0:
```python
import jax
import jax.numpy as jnp
from jax import lax
from jax.sharding import PartitionSpec as P

loss_scale = 64.0


def body(hidden_ref, hidden_train, head_ref, head_train, targets, mask):
    vocab_rows = head_train.shape[0]
    tok_rows = hidden_train.shape[0]
    selected = tok_rows * 5 // 8
    offset = lax.axis_index("vocab") * vocab_rows
    contract_last = (((1,), (1,)), ((), ()))
    columns = hidden_ref
    ref_logits = lax.dot_general(
        columns,
        lax.all_gather(head_ref, "dp", axis=1, tiled=True),
        contract_last,
        preferred_element_type=jnp.float32,
    )
    trained_slab = lax.all_gather(head_train, "dp", axis=1, tiled=True)
    logits = lax.dot_general(
        hidden_train, trained_slab, contract_last, preferred_element_type=jnp.float32
    )
    target_hit = (
        lax.broadcasted_iota(jnp.int32, (tok_rows, vocab_rows), 1) + offset == targets[:, None]
    )
    ref_pick = jnp.sum(jnp.where(target_hit, ref_logits, 0.0), axis=1)
    train_pick = jnp.sum(jnp.where(target_hit, logits, 0.0), axis=1)
    local_ref_max = jnp.max(ref_logits, axis=1)
    local_train_max = jnp.max(logits, axis=1)
    ref_max, train_max = lax.pmax((local_ref_max, local_train_max), "vocab")
    ref_sum, train_sum, ref_target, train_target = lax.psum(
        (
            jnp.sum(jnp.exp(ref_logits - ref_max[:, None]), axis=1),
            jnp.sum(jnp.exp(logits - train_max[:, None]), axis=1),
            ref_pick,
            train_pick,
        ),
        "vocab",
    )
    ce_ref = jnp.log(ref_sum) + ref_max - ref_target
    ce_train = jnp.log(train_sum) + train_max - train_target
    excess = ce_train - ce_ref
    select_weight = mask.astype(jnp.float32)
    total_sum = lax.psum(jnp.sum(select_weight * ce_train), "dp")
    loss_value = total_sum / (lax.axis_size("dp") * selected)
    probabilities = jnp.exp(logits - train_max[:, None]) / train_sum[:, None]
    logit_grads = (
        loss_scale * select_weight[:, None] * (probabilities - target_hit.astype(jnp.float32))
    ).astype(jnp.bfloat16)
    chosen_rows = jnp.argsort(1 - mask, stable=True)[:selected]
    chosen_grads = logit_grads[chosen_rows]
    columns = trained_slab
    grad_piece = lax.psum_scatter(
        lax.dot_general(
            columns, chosen_grads, (((0,), (1,)), ((), ())), preferred_element_type=jnp.float32
        ),
        "vocab",
        scatter_dimension=0,
        tiled=True,
    )
    hidden_grad = (
        jnp.zeros((grad_piece.shape[0], tok_rows), jnp.float32).at[:, chosen_rows].set(grad_piece)
    )
    return (excess, loss_value, hidden_grad)


def solution(mesh):
    in_specs = (P("dp", None), P("dp", None), P("vocab", "dp"), P("vocab", "dp"), P("dp"), P("dp"))
    out_specs = (P("dp"), P(), P("vocab", "dp"))
    return jax.shard_map(body, mesh=mesh, in_specs=in_specs, out_specs=out_specs, check_vma=False)
```

profile of v0, /device:TPU:1, one launch (start us, length us, event | category | flops | bytes accessed | tf_op | source)
XLA Modules:
  0.0 621.5 jit_solution(12017977315306434523)
XLA Ops:
  7.2 0.0 copy-start
  7.2 0.0 all-gather.5.cloned.1.call-start
  7.2 0.7 all-gather.5.cloned.1.call-update
  7.9 0.0 all-gather.3.cloned.1.call-start
  8.0 0.7 all-gather.3.cloned.1.call-update
  8.7 0.0 reduce-scatter.4.cloned.1.call-start
  8.7 0.7 broadcast_subtract_fusion
  9.4 3.2 sort.17
  12.6 0.0 copy-start.2
  12.6 99.4 %all-gather.5.cloned.1.call-done = bf16[1008,4096]{1,0:T(8,128)(2,1)} async-done(((bf16[1008,512]{1,0:T(8,128)(2,1)}), bf16[1008,4096]{1,0:T(8,128)(2,1)}) %all-gather.5.cloned.1.call-update) | async-done | bytes 8257552 | tf_op jit(solution)/shard_map/all_gather | solution.py:18
  112.0 0.0 copy-done
  112.0 6.2 fusion.9
  118.2 0.0 copy-start.1
  118.2 90.3 %all-gather.3.cloned.1.call-done = bf16[1008,4096]{1,0:T(8,128)(2,1)} async-done(((bf16[1008,512]{1,0:T(8,128)(2,1)}), bf16[1008,4096]{1,0:T(8,128)(2,1)}) %all-gather.3.cloned.1.call-update) | async-done | bytes 8257552 | tf_op jit(solution)/shard_map/all_gather | solution.py:22
  208.5 6.6 %fusion.10 = (f32[160]{0:T(256)S(1)}, f32[160,1008]{1,0:T(8,128)S(1)}) fusion(bf16[160,4096]{1,0:T(8,128)(2,1)} %param.7, bf16[1008,4096]{1,0:T(8,128)(2,1)} %all-gather.3.cloned.1.call-done), kind=kOutput, calls=%fused_computation.26 | convolution fusion | flops 1321366912 | bytes 10214016 | tf_op jit(solution)/shard_map/dot_general | solution.py:23
  215.1 124.1 %all-reduce.1 = (f32[160]{0:T(256)S(1)}, f32[160]{0:T(256)S(1)}) all-reduce(f32[160]{0:T(256)S(1)} %get-tuple-element.26, f32[160]{0:T(256)S(1)} %get-tuple-element.28), channel_id=1, replica_groups=mesh['dp'=8,'vocab'=64] {'vocab'}, use_global_device_ids=true, to_apply=%region_7.8 | all-reduce | flops 320 | bytes 2560 | tf_op jit(solution)/shard_map/pmax | solution.py:33
  339.2 0.0 copy-done.2
  339.2 0.5 fusion.5
  339.7 128.4 %all-reduce = (f32[160]{0:T(256)S(1)}, f32[160]{0:T(256)S(1)}, f32[160]{0:T(256)S(1)}, f32[160]{0:T(256)S(1)}) all-reduce(f32[160]{0:T(256)S(1)} %get-tuple-element.21, f32[160]{0:T(256)S(1)} %get-tuple-element.22, f32[160]{0:T(256)S(1)} %get-tuple-element.12, ...), channel_id=1, replica_groups=mesh['dp'=8,'vocab'=64] {'vocab'}, use_global_device_ids=true, to_apply=%region_11.12 | all-reduce | flops 640 | bytes 5120 | tf_op jit(solution)/shard_map/psum | solution.py:34
  468.2 0.0 copy-done.1
  468.2 1.2 multiply_reduce_fusion
  469.3 0.3 fusion.4
  469.6 0.8 gather_fusion
  470.4 4.7 convolution_bitcast_fusion
  475.1 1.9 copy.11
  477.0 0.0 reduce-scatter.4.cloned.1.call-update
  477.0 12.6 %psum.39 = f32[]{:T(128)} all-reduce(f32[]{:T(128)} %get-tuple-element.23), channel_id=1, replica_groups=mesh['dp'=8,'vocab'=64] {'dp'}, use_global_device_ids=true, to_apply=%region_13.14 | all-reduce | flops 1 | bytes 8 | tf_op jit(solution)/shard_map/psum | solution.py:47
  490.3 121.2 %reduce-scatter.4.cloned.1.call-done = f32[64,100]{1,0:T(8,128)} async-done(((f32[4096,100]{1,0:T(8,128)}), f32[64,100]{1,0:T(8,128)}) %reduce-scatter.4.cloned.1.call-update) | async-done | bytes 25616
  611.5 0.9 copy.12
  612.3 0.8 scatter_custom_fusion
  613.1 0.7 copy.10
  (4 shorter events, 0.0 us)
Async XLA Ops:
  7.2 104.8 %copy-start = (bf16[160,4096]{1,0:T(8,128)(2,1)S(1)}, bf16[160,4096]{1,0:T(8,128)(2,1)}, u32[]{:S(2)}) copy-start(bf16[160,4096]{1,0:T(8,128)(2,1)} %param.6) | copy-start | bytes 3932164
  7.2 104.8 %all-gather.5.cloned.1.call-start = ((), (), s32[]{:S(2)}) async-start(), calls=%async_computation.2 | async-start | bytes 9289728 | tf_op jit(solution)/shard_map/all_gather | solution.py:18
  7.9 200.6 %all-gather.3.cloned.1.call-start = ((), (), s32[]{:S(2)}) async-start(), calls=%async_computation.1 | async-start | bytes 9289728 | tf_op jit(solution)/shard_map/all_gather | solution.py:22
  8.7 602.8 %reduce-scatter.4.cloned.1.call-start = ((), (), s32[]{:S(2)}) async-start(), calls=%async_computation.3 | async-start | bytes 2129920
  12.6 326.7 %copy-start.2 = (s32[160]{0:T(256)S(1)}, s32[160]{0:T(256)}, u32[]{:S(2)}) copy-start(s32[160]{0:T(256)} %param.10) | copy-start | bytes 1924
  118.2 350.0 %copy-start.1 = (s32[160]{0:T(256)S(1)}, s32[160]{0:T(256)}, u32[]{:S(2)}) copy-start(s32[160]{0:T(256)} %param.11) | copy-start | bytes 1924
Sparse Core Ops, SparseCore 0:
  10.1 101.8 all-gather.4
  114.1 94.4 all-gather.2
  477.1 134.2 reduce-scatter.3
where the time goes:
time: 626 us; the launch traced here: 622 us
  waiting for transfers between devices  312 us (50%)
  blocking collectives  265 us (42%)
  matrix products  17.5 us (3%)
  between operations  15.6 us (2%)
    psum x1, blocking collectives, body(): lax.psum((jnp.sum(jnp.exp(ref_logits - ref_max[:, None]), axis=1), jnp.su...  128 us
    pmax x1, blocking collectives, body(): ref_max, train_max = lax.pmax((local_ref_max, local_train_max), 'vocab')  124 us
    unnamed x4, waiting for transfers between devices  123 us
    all_gather x1, waiting for transfers between devices, body(): lax.all_gather(head_ref, 'dp', axis=1, tiled=True)  99.4 us
    all_gather x1, waiting for transfers between devices, body(): trained_slab = lax.all_gather(head_train, 'dp', axis=1, tiled=True)  90.3 us
    psum x1, blocking collectives, body(): total_sum = lax.psum(jnp.sum(select_weight * ce_train), 'dp')  12.6 us
  transfers between devices with their start and end apart: 3, of which 3 were waited for; matrix products, arithmetic and copies ran while one was open for 2% of the time, Pallas kernels for 0%

commit v1 on v0

v1 whole, which is shorter than its diff:
```python
import functools

import jax
import jax.numpy as jnp
from jax import lax
from jax.experimental import pallas as pl
from jax.experimental.pallas import tpu as pltpu
from jax.sharding import PartitionSpec as P

MESH = pl.DeviceIdType.MESH
NX, NY, NZ = 4, 8, 8
loss_scale = 64.0
TOK = 160
SEL = 100
SLOT = 112
ROWS = 128
PIECE = 128
FEAT = 512
FAR_FIRST = (4, 3, 5, 2, 6, 1, 7)
NEAR_FIRST = (1, 7, 2, 6, 3, 5, 4)


def coords():
    z = lax.axis_index("dp")
    v = lax.axis_index("vocab")
    return v // 16, (v // 2) % NY, z, v % 2


def vocab_index(x, y, c):
    return (x * NY + y) * 2 + c


def greet(devices):
    barrier = pltpu.get_barrier_semaphore()
    for device in devices:
        pl.semaphore_signal(barrier, inc=1, device_id=device, device_id_type=MESH)
    pl.semaphore_wait(barrier, len(devices))


def remote(src, dst, send_sem, recv_sem, device):
    return pltpu.make_async_remote_copy(
        src_ref=src, dst_ref=dst, send_sem=send_sem, recv_sem=recv_sem,
        device_id=device, device_id_type=MESH,
    )


class Ring:
    def __init__(self, buf, pos, size, width, right, left, active, send_sem, recv_sem):
        self.buf, self.pos, self.size, self.width = buf, pos, size, width
        self.devices = (right, left)
        self.active, self.send_sem, self.recv_sem = active, send_sem, recv_sem

    def copy(self, step, way, slot, arriving):
        back = step if arriving else step - 1
        sign = -1 if way == 0 else 1
        block = (self.pos + sign * back + self.size) % self.size
        column = pl.multiple_of(block * self.width, self.width)
        part = self.buf.at[pl.ds(TOK * slot, TOK), pl.ds(column, self.width)]
        return remote(
            part, part, self.send_sem.at[step - 1, way, slot],
            self.recv_sem.at[step - 1, way, slot], self.devices[way],
        )

    def ways(self, step, slot):
        if 2 * step < self.size:
            return (0, 1)
        return (0,) if slot < 2 else (1,)

    def send(self, step, slot):
        @pl.when(self.active(slot))
        def _():
            for way in self.ways(step, slot):
                self.copy(step, way, slot, False).start()

    def wait(self, step, slot):
        @pl.when(self.active(slot))
        def _():
            for way in self.ways(step, slot):
                self.copy(step, way, slot, True).wait_recv()

    def drain(self):
        for slot in range(4):
            @pl.when(self.active(slot))
            def _():
                for step in range(1, self.size // 2 + 1):
                    for way in self.ways(step, slot):
                        self.copy(step, way, slot, False).wait_send()


def spread_kernel(
    hid_ref, hid_train, head_ref, head_train, meta,
    x_ref, x_train, g_ref, g_train, meta_all,
    local_sem, z_send, z_recv, m_send, m_recv, w_send, w_recv, s_send, s_recv,
    ra_send, ra_recv, rb_send, rb_recv, ta_send, ta_recv, tb_send, tb_recv,
):
    x, y, z, c = coords()
    v = vocab_index(x, y, c)
    sibling = (z, vocab_index(x, y, 1 - c))
    x_right = (z, vocab_index((x + 1) % NX, y, c))
    x_left = (z, vocab_index((x + NX - 1) % NX, y, c))
    y_right = (z, vocab_index(x, (y + 1) % NY, c))
    y_left = (z, vocab_index(x, (y + NY - 1) % NY, c))
    peers = {s: ((z + s) % NZ, v) for s in range(1, NZ)}
    greet([peers[s] for s in range(1, NZ)] + [sibling, x_right, x_left, y_right, y_left])

    own_slot = z % 4
    is_source = z // 4 == c

    def active(slot):
        return z != 4 * c + slot

    hid = (hid_ref, hid_train)
    wide = (x_ref, x_train)
    heads = (head_ref, head_train)
    got = (g_ref, g_train)
    piece_at = (
        pl.multiple_of((y * NX + x) * PIECE, PIECE),
        pl.multiple_of((x * NY + y) * PIECE, PIECE),
    )

    def z_copy(a, slot, s):
        return remote(
            hid[a].at[:, pl.ds(piece_at[a], PIECE)],
            wide[a].at[pl.ds(pl.multiple_of(TOK * slot, 16), TOK), pl.ds(piece_at[a], PIECE)],
            z_send.at[a, s - 1], z_recv.at[a, slot], peers[s],
        )

    def own_copy(a):
        return pltpu.make_async_copy(
            hid[a],
            wide[a].at[pl.ds(pl.multiple_of(TOK * own_slot, 16), TOK), :],
            local_sem.at[a],
        )

    @pl.when(is_source)
    def _():
        for a in (1, 0):
            for s in FAR_FIRST:
                z_copy(a, own_slot, s).start()
        for a in (0, 1):
            own_copy(a).start()

    def meta_copy(s, arriving):
        source = (z + NZ - s) % NZ if arriving else z
        return remote(
            meta, meta_all.at[source], m_send.at[s - 1], m_recv.at[s - 1], peers[s]
        )

    own_meta = pltpu.make_async_copy(meta, meta_all.at[z], local_sem.at[2])
    own_meta.start()
    for s in range(1, NZ):
        meta_copy(s, False).start()

    def row_block(j):
        return pl.multiple_of(j * ROWS - 16 * (j // 7), 16)

    mine = pl.ds(pl.multiple_of(ROWS * c, ROWS), ROWS)

    def part_of(a, source):
        return got[a].at[mine, pl.ds(pl.multiple_of(source * FEAT, FEAT), FEAT)]

    def head_copy(a, s, arriving):
        dest = (z + s) % NZ
        source = (z + NZ - s) % NZ if arriving else z
        return remote(
            heads[a].at[pl.ds(row_block(dest), ROWS), :], part_of(a, source),
            w_send.at[a, s - 1], w_recv.at[a, s - 1], peers[s],
        )

    def share_copy(a, s):
        part = part_of(a, (z + NZ - s) % NZ)
        return remote(part, part, s_send.at[a, s], s_recv.at[a, s], sibling)

    def share_arriving(a, s):
        source = (z + NZ - s) % NZ
        part = got[a].at[
            pl.ds(pl.multiple_of(ROWS * (1 - c), ROWS), ROWS),
            pl.ds(pl.multiple_of(source * FEAT, FEAT), FEAT),
        ]
        return remote(part, part, s_send.at[a, s], s_recv.at[a, s], sibling)

    own_rows = [
        pltpu.make_async_copy(
            heads[a].at[pl.ds(row_block(z), ROWS), :], part_of(a, z), local_sem.at[3 + a]
        )
        for a in (0, 1)
    ]
    for a in (1, 0):
        own_rows[a].start()
        for s in FAR_FIRST:
            head_copy(a, s, False).start()

    ra = Ring(x_ref, y * NX + x, NX, PIECE, x_right, x_left, active, ra_send, ra_recv)
    rb = Ring(x_ref, y, NY, NX * PIECE, y_right, y_left, active, rb_send, rb_recv)
    ta = Ring(x_train, x * NY + y, NY, PIECE, y_right, y_left, active, ta_send, ta_recv)
    tb = Ring(x_train, x, NX, NY * PIECE, x_right, x_left, active, tb_send, tb_recv)
    ra_base, ta_base = y * NX, x * NY
    ra.pos, ta.pos = x, y

    def first_stage(ring, base):
        def copy(step, way, slot, arriving):
            back = step if arriving else step - 1
            sign = -1 if way == 0 else 1
            block = base + (ring.pos + sign * back + ring.size) % ring.size
            part = ring.buf.at[
                pl.ds(TOK * slot, TOK), pl.ds(pl.multiple_of(block * PIECE, PIECE), PIECE)
            ]
            return remote(
                part, part, ring.send_sem.at[step - 1, way, slot],
                ring.recv_sem.at[step - 1, way, slot], ring.devices[way],
            )
        ring.copy = copy

    first_stage(ra, ra_base)
    first_stage(ta, ta_base)

    slots = range(4)
    for slot in slots:
        for a, ring in ((1, ta), (0, ra)):
            @pl.when(active(slot))
            def _():
                z_copy(a, slot, 1).wait_recv()
            ring.send(1, slot)

    def advance(*moves):
        for slot in slots:
            for ring, step, after, after_step in moves:
                ring.wait(step, slot)
                if after is not None:
                    after.send(after_step, slot)

    advance((ta, 1, ta, 2), (ra, 1, ra, 2))
    advance((ta, 2, ta, 3), (ra, 2, rb, 1))
    advance((ta, 3, ta, 4))
    advance((ta, 4, tb, 1))
    for a in (1, 0):
        own_rows[a].wait()
        share_copy(a, 0).start()
    advance((rb, 1, rb, 2))
    for s in (1, 7, 2, 6):
        head_copy(1, s, True).wait_recv()
        share_copy(1, s).start()
    advance((rb, 2, rb, 3), (tb, 1, tb, 2))
    for s in (3, 5, 4):
        head_copy(1, s, True).wait_recv()
        share_copy(1, s).start()
    advance((rb, 3, rb, 4))
    for s in NEAR_FIRST:
        head_copy(0, s, True).wait_recv()
        share_copy(0, s).start()
    advance((tb, 2, None, 0), (rb, 4, None, 0))

    own_meta.wait()
    for s in range(1, NZ):
        meta_copy(s, True).wait_recv()
    for a in (1, 0):
        for s in range(NZ):
            share_arriving(a, s).wait_recv()

    @pl.when(is_source)
    def _():
        for a in (0, 1):
            own_copy(a).wait()
            for s in range(1, NZ):
                z_copy(a, own_slot, s).wait_send()

    for s in range(1, NZ):
        meta_copy(s, False).wait_send()
    for a in (0, 1):
        for s in range(1, NZ):
            head_copy(a, s, False).wait_send()
        for s in range(NZ):
            share_copy(a, s).wait_send()
    for ring in (ra, rb, ta, tb):
        ring.drain()


def spread(hidden_ref, hidden_train, head_ref, head_train, meta):
    anywhere = pl.BlockSpec(memory_space=pl.ANY)
    dma = pltpu.SemaphoreType.DMA
    half = 4 * TOK
    width = hidden_ref.shape[1]
    sds = jax.ShapeDtypeStruct
    return pl.pallas_call(
        spread_kernel,
        out_shape=[
            sds((half, width), jnp.bfloat16), sds((half, width), jnp.bfloat16),
            sds((2 * ROWS, width), jnp.bfloat16), sds((2 * ROWS, width), jnp.bfloat16),
            sds((NZ,) + meta.shape, meta.dtype),
        ],
        in_specs=[anywhere] * 5,
        out_specs=[anywhere] * 5,
        scratch_shapes=[
            dma((5,)), dma((2, NZ - 1)), dma((2, 4)), dma((NZ - 1,)), dma((NZ - 1,)),
            dma((2, NZ - 1)), dma((2, NZ - 1)), dma((2, NZ)), dma((2, NZ)),
            dma((2, 2, 4)), dma((2, 2, 4)), dma((4, 2, 4)), dma((4, 2, 4)),
            dma((4, 2, 4)), dma((4, 2, 4)), dma((2, 2, 4)), dma((2, 2, 4)),
        ],
        compiler_params=pltpu.CompilerParams(collective_id=0, has_side_effects=True),
        name="spread",
    )(hidden_ref, hidden_train, head_ref, head_train, meta)


def merge(blocks):
    out = []
    for base in (0, 3):
        tops = [b[base:base + 1, :] for b in blocks]
        top = functools.reduce(jnp.maximum, tops)
        total = sum(b[base + 1:base + 2, :] * jnp.exp(t - top) for b, t in zip(blocks, tops))
        picked = sum(b[base + 2:base + 3, :] for b in blocks)
        out += [top, total, picked]
    return out


def stats_kernel(mine, out, acc, zbuf, xbuf, ybuf, z_send, z_recv, x_send, x_recv,
                 y_send, y_recv, c_send, c_recv):
    x, y, z, c = coords()
    v = vocab_index(x, y, c)
    sibling = (z, vocab_index(x, y, 1 - c))
    z_peers = [((z + s) % NZ, v) for s in range(1, NZ)]
    x_peers = [(z, vocab_index((x + s) % NX, y, c)) for s in range(1, NX)]
    y_peers = [(z, vocab_index(x, (y + s) % NY, c)) for s in range(1, NY)]
    greet(z_peers + x_peers + y_peers + [sibling])

    source = mine
    level = 0
    pending = []
    for peers, buf, send, recv in (
        (z_peers, zbuf, z_send, z_recv),
        (x_peers, xbuf, x_send, x_recv),
        (y_peers, ybuf, y_send, y_recv),
    ):
        copies = [
            remote(source, buf.at[s], send.at[s], recv.at[s], peer)
            for s, peer in enumerate(peers)
        ]
        for copy in copies:
            copy.start()
        for copy in copies:
            copy.wait_recv()
        parts = merge([source[...]] + [buf[s] for s in range(len(peers))])
        if level < 2:
            target = acc.at[level]
            for row, part in enumerate(parts):
                target[row:row + 1, :] = part
            target[6:8, :] = jnp.zeros_like(target[6:8, :])
            source = target
        pending += copies
        level += 1
    for row, part in enumerate(parts):
        out[c, row:row + 1, :] = part
    out[c, 6:8, :] = jnp.zeros((2, mine.shape[1]), jnp.float32)
    share = remote(out.at[c], out.at[c], c_send, c_recv, sibling)
    share.start()
    remote(out.at[1 - c], out.at[1 - c], c_send, c_recv, sibling).wait_recv()
    share.wait_send()
    for copy in pending:
        copy.wait_send()


def exchange_stats(stats):
    vmem = pl.BlockSpec(memory_space=pltpu.VMEM)
    dma = pltpu.SemaphoreType.DMA
    shape = stats.shape
    return pl.pallas_call(
        stats_kernel,
        out_shape=jax.ShapeDtypeStruct((2,) + shape, jnp.float32),
        in_specs=[vmem],
        out_specs=vmem,
        scratch_shapes=[
            pltpu.VMEM((2,) + shape, jnp.float32), pltpu.VMEM((NZ - 1,) + shape, jnp.float32),
            pltpu.VMEM((NX - 1,) + shape, jnp.float32), pltpu.VMEM((NY - 1,) + shape, jnp.float32),
            dma((NZ - 1,)), dma((NZ - 1,)), dma((NX - 1,)), dma((NX - 1,)),
            dma((NY - 1,)), dma((NY - 1,)), dma, dma,
        ],
        compiler_params=pltpu.CompilerParams(collective_id=1, has_side_effects=True),
        name="stats",
    )(stats)


def gather_kernel(part, out, local_sem, c_send, c_recv, r_send, r_recv):
    x, y, z, c = coords()
    v = vocab_index(x, y, c)
    sibling = (z, vocab_index(x, y, 1 - c))
    devices = (((z + 1) % NZ, v), ((z + NZ - 1) % NZ, v))
    greet([devices[0], devices[1], sibling])
    half = part.shape[0]

    def place(h, block):
        return out.at[
            pl.ds(pl.multiple_of(h * half, 16), half),
            pl.ds(pl.multiple_of(block * ROWS, ROWS), ROWS),
        ]

    def columns(k):
        return part.at[:, pl.ds(pl.multiple_of(k * ROWS, ROWS), ROWS)]

    local = pltpu.make_async_copy(columns(c), place(c, z), local_sem)
    share = remote(columns(1 - c), place(c, z), c_send, c_recv, sibling)
    share.start()
    local.start()

    def ring(step, way, index, arriving):
        h = c if index == 0 else 1 - c
        back = step if arriving else step - 1
        sign = -1 if way == 0 else 1
        block = (z + sign * back + NZ) % NZ
        src = place(h, block)
        if step == 1 and index == 0 and not arriving:
            src = columns(c)
        return remote(
            src, place(h, block), r_send.at[step - 1, way, index],
            r_recv.at[step - 1, way, index], devices[way],
        )

    def ways(step, index):
        return (0, 1) if step < 4 else (index,)

    for way in (0, 1):
        ring(1, way, 0, False).start()
    remote(columns(c), place(1 - c, z), c_send, c_recv, sibling).wait_recv()
    for way in (0, 1):
        ring(1, way, 1, False).start()
    for step in (1, 2, 3):
        for index in (0, 1):
            for way in (0, 1):
                ring(step, way, index, True).wait_recv()
                if way in ways(step + 1, index):
                    ring(step + 1, way, index, False).start()
    for index in (0, 1):
        ring(4, index, index, True).wait_recv()
    local.wait()
    share.wait_send()
    for step in (1, 2, 3, 4):
        for index in (0, 1):
            for way in ways(step, index):
                ring(step, way, index, False).wait_send()


def gather_grads(part):
    anywhere = pl.BlockSpec(memory_space=pl.ANY)
    dma = pltpu.SemaphoreType.DMA
    return pl.pallas_call(
        gather_kernel,
        out_shape=jax.ShapeDtypeStruct((2 * part.shape[0], NZ * ROWS), part.dtype),
        in_specs=[anywhere],
        out_specs=anywhere,
        scratch_shapes=[dma, dma, dma, dma((4, 2, 2)), dma((4, 2, 2))],
        compiler_params=pltpu.CompilerParams(collective_id=2, has_side_effects=True),
        name="gather_grads",
    )(part)


def reduce_kernel(grad, out, cbuf, acc, xbuf, bsum, ybuf, csum, c_send, c_recv,
                  x_send, x_recv, y_send, y_recv, f_send, f_recv, f_local):
    x, y, z, c = coords()
    v = vocab_index(x, y, c)
    sibling = (z, vocab_index(x, y, 1 - c))
    x_peers = [(z, vocab_index((x + s) % NX, y, c)) for s in range(1, NX)]
    y_peers = [(z, vocab_index(x, (y + s) % NY, c)) for s in range(1, NY)]
    dest = (4 * c + y // 2, 8 * z + 2 * x + y % 2)
    j = v % 8
    origin = (v // 8, vocab_index(j // 2, (z % 4) * 2 + j % 2, z // 4))
    stays = jnp.logical_and(dest[0] == z, dest[1] == v)
    leaves = jnp.logical_not(stays)

    barrier = pltpu.get_barrier_semaphore()
    for device in x_peers + y_peers + [sibling]:
        pl.semaphore_signal(barrier, inc=1, device_id=device, device_id_type=MESH)

    @pl.when(leaves)
    def _():
        for device in (dest, origin):
            pl.semaphore_signal(barrier, inc=1, device_id=device, device_id_type=MESH)

    greeted = len(x_peers) + len(y_peers) + 1
    pl.semaphore_wait(barrier, greeted + 2 - 2 * stays.astype(jnp.int32))

    lanes = pl.ds(pl.multiple_of(512 * c, 512), 512)
    other_lanes = pl.ds(pl.multiple_of(512 * (1 - c), 512), 512)

    def rows(q):
        return pl.ds(pl.multiple_of(q * 128, 128), 128)

    order = [(x + s) % NX for s in (2, 1, 3, 0)]
    shares = [
        remote(grad.at[rows(q), other_lanes], cbuf.at[rows(q), :], c_send.at[k], c_recv.at[k], sibling)
        for k, q in enumerate(order)
    ]
    for share in shares:
        share.start()
    x_copies = []
    for k, s in enumerate((2, 1, 3, 0)):
        q = order[k]
        shares[k].wait_recv()
        acc[rows(q), :] = grad[rows(q), lanes] + cbuf[rows(q), :]
        if s:
            copy = remote(
                acc.at[rows(q), :], xbuf.at[s - 1], x_send.at[s - 1], x_recv.at[s - 1],
                x_peers[s - 1],
            )
            copy.start()
            x_copies.append(copy)
    for copy in x_copies:
        copy.wait_recv()
    bsum[...] = acc[rows(x), :] + xbuf[0] + xbuf[1] + xbuf[2]

    def piece(q):
        return (
            pl.ds(pl.multiple_of((q % 2) * 64, 64), 64),
            pl.ds(pl.multiple_of((q // 2) * 128, 128), 128),
        )

    y_copies = []
    for s in FAR_FIRST:
        a, b = piece((y + s) % NY)
        copy = remote(
            bsum.at[a, b], ybuf.at[s - 1], y_send.at[s - 1], y_recv.at[s - 1], y_peers[s - 1]
        )
        copy.start()
        y_copies.append(copy)
    for copy in y_copies:
        copy.wait_recv()
    a, b = piece(y)
    csum[...] = bsum[a, b] + sum(ybuf[s] for s in range(NY - 1))

    final = remote(csum, out, f_send, f_recv, dest)
    stay = pltpu.make_async_copy(csum, out, f_local)

    @pl.when(leaves)
    def _():
        final.start()
        final.wait_recv()
        final.wait_send()

    @pl.when(stays)
    def _():
        stay.start()
        stay.wait()

    for copy in shares + x_copies + y_copies:
        copy.wait_send()


def reduce_grads(grad):
    vmem = pl.BlockSpec(memory_space=pltpu.VMEM)
    dma = pltpu.SemaphoreType.DMA
    f32 = jnp.float32
    return pl.pallas_call(
        reduce_kernel,
        out_shape=jax.ShapeDtypeStruct((64, 128), f32),
        in_specs=[vmem],
        out_specs=vmem,
        scratch_shapes=[
            pltpu.VMEM((512, 512), f32), pltpu.VMEM((512, 512), f32),
            pltpu.VMEM((NX - 1, 128, 512), f32), pltpu.VMEM((128, 512), f32),
            pltpu.VMEM((NY - 1, 64, 128), f32), pltpu.VMEM((64, 128), f32),
            dma((4,)), dma((4,)), dma((NX - 1,)), dma((NX - 1,)),
            dma((NY - 1,)), dma((NY - 1,)), dma, dma, dma,
        ],
        compiler_params=pltpu.CompilerParams(
            collective_id=3, has_side_effects=True, vmem_limit_bytes=24 * 1024 * 1024
        ),
        name="reduce_grads",
    )(grad)


def body(hidden_ref, hidden_train, head_ref, head_train, targets, mask):
    f32 = jnp.float32
    vocab_rows = head_train.shape[0]
    x, y, z, c = coords()
    chip = lax.axis_index("vocab") // 2
    contract_last = (((1,), (1,)), ((), ()))

    meta = jnp.zeros((8, 256), jnp.int32)
    meta = meta.at[0, :TOK].set(targets).at[1, :TOK].set(mask)
    x_ref, x_train, g_ref, g_train, meta_all = spread(
        hidden_ref, hidden_train, head_ref, head_train, meta
    )
    targets_all = meta_all[:, 0, :TOK]
    mask_all = meta_all[:, 1, :TOK]
    half_targets = lax.dynamic_slice_in_dim(targets_all, 4 * c, 4, 0).reshape(4 * TOK)
    half_mask = lax.dynamic_slice_in_dim(mask_all, 4 * c, 4, 0)

    train_logits = lax.dot_general(x_train, g_train, contract_last, preferred_element_type=f32)
    ref_logits = lax.dot_general(x_ref, g_ref, contract_last, preferred_element_type=f32)

    column = jnp.arange(2 * ROWS, dtype=jnp.int32)
    start = z * ROWS - 16 * (z // 7)
    row_id = (2 * chip + column // ROWS) * vocab_rows + start + column % ROWS
    valid = jnp.logical_or(z < 7, column % ROWS >= 16)
    hit = jnp.logical_and(row_id[None, :] == half_targets[:, None], valid[None, :])

    def local_stats(logits):
        top = jnp.max(jnp.where(valid[None, :], logits, -jnp.inf), axis=1)
        total = jnp.sum(jnp.where(valid[None, :], jnp.exp(logits - top[:, None]), 0.0), axis=1)
        picked = jnp.sum(jnp.where(hit, logits, 0.0), axis=1)
        return [top, total, picked]

    zeros = jnp.zeros((4 * TOK,), f32)
    stats = jnp.stack(local_stats(ref_logits) + local_stats(train_logits) + [zeros, zeros])
    both = exchange_stats(stats)

    ce_ref = jnp.log(both[:, 1]) + both[:, 0] - both[:, 2]
    ce_train = jnp.log(both[:, 4]) + both[:, 3] - both[:, 5]
    excess_all = (ce_train - ce_ref).reshape(NZ, TOK)
    excess = lax.dynamic_slice_in_dim(excess_all, z, 1, 0).reshape(TOK)
    weight_all = mask_all.astype(f32)
    loss_value = jnp.sum(weight_all * ce_train.reshape(NZ, TOK)) / (NZ * SEL)

    own = lax.dynamic_slice_in_dim(both, c, 1, 0)[0]
    probabilities = jnp.exp(train_logits - own[3][:, None]) / own[4][:, None]
    logit_grads = jnp.where(
        valid[None, :], loss_scale * (probabilities - hit.astype(f32)), 0.0
    ).astype(jnp.bfloat16)

    rank = jnp.cumsum(half_mask, axis=1) - 1
    pick = jnp.logical_and(
        rank[:, None, :] == jnp.arange(SLOT, dtype=jnp.int32)[None, :, None],
        half_mask[:, None, :] != 0,
    ).astype(jnp.bfloat16)
    chosen = lax.dot_general(
        pick, logit_grads.reshape(4, TOK, 2 * ROWS), (((2,), (1,)), ((0,), (0,))),
        preferred_element_type=f32,
    ).astype(jnp.bfloat16).reshape(4 * SLOT, 2 * ROWS)

    grads = gather_grads(chosen)
    slotted = jnp.pad(grads.reshape(NZ, SLOT, NZ * ROWS), ((0, 0), (0, 128 - SLOT), (0, 0)))
    slotted = slotted.reshape(NZ * 128, NZ * ROWS)
    home = jnp.concatenate([head_train[:7 * ROWS], head_train[7 * ROWS - 16:]], axis=0)
    partial_grad = lax.dot_general(
        home, slotted, (((0,), (1,)), ((), ())), preferred_element_type=f32
    )
    piece = reduce_grads(partial_grad)

    own_rank = jnp.cumsum(mask) - 1
    place = jnp.logical_and(
        jnp.arange(128, dtype=jnp.int32)[:, None] == own_rank[None, :], mask[None, :] != 0
    ).astype(f32)
    hidden_grad = lax.dot_general(
        piece, place, (((1,), (0,)), ((), ())), precision=lax.Precision.HIGHEST,
        preferred_element_type=f32,
    )
    return (excess, loss_value, hidden_grad)


def solution(mesh):
    in_specs = (P("dp", None), P("dp", None), P("vocab", "dp"), P("vocab", "dp"), P("dp"), P("dp"))
    out_specs = (P("dp"), P(), P("vocab", "dp"))
    return jax.shard_map(body, mesh=mesh, in_specs=in_specs, out_specs=out_specs, check_vma=False)
```

time: 626 us -> 233 us (0.37)
  waiting for transfers between devices: 312 us -> 0 us
  blocking collectives: 265 us -> 0 us
  Pallas kernels: 0 us -> 205 us
  between operations: 15.6 us -> 2.74 us
    pallas_call x0 -> x4, Pallas kernels: none -> 205 us  [the longest x1 121 us: spread(): pl.pallas_call(spread_kernel, out_shape=[sds((half, width), jnp.bfloat16)...]
    all_gather x2 -> x0, waiting for transfers between devices: 190 us -> none  [the longest x1 99.4 us: body(): lax.all_gather(head_ref, 'dp', axis=1, tiled=True)]
    psum x2 -> x0, blocking collectives: 141 us -> none  [the longest x1 128 us: body(): lax.psum((jnp.sum(jnp.exp(ref_logits - ref_max[:, None]), axis=1), jnp.su...]
    pmax x1 -> x0, blocking collectives: 124 us -> none  [body(): ref_max, train_max = lax.pmax((local_ref_max, local_train_max), 'vocab')]
    unnamed x4 -> x0, waiting for transfers between devices: 123 us -> none
    dot_general x3 -> x5, matrix products: 17.5 us -> 12.8 us  [the longest x1 5.12 us: body(): lax.dot_general(x_ref, g_ref, contract_last, preferred_element_type=f32)]
  transfers between devices with their start and end apart: 3 -> 0, of which waited for: 3 -> 0; matrix products, arithmetic and copies ran while one was open for 2% -> 0% of each run, Pallas kernels for 0% -> 0%
where the time goes in v1:
time: 233 us; the launch traced here: 231 us
  Pallas kernels  205 us (88%)
  matrix products  12.8 us (5%)
  local copies, waits for them, and re-layouts  6.36 us (3%)
  other arithmetic  4.74 us (2%)
  between operations  2.74 us (1%)
    pallas_call x1, Pallas kernels, spread(): pl.pallas_call(spread_kernel, out_shape=[sds((half, width), jnp.bfloat16)...  121 us
    pallas_call x1, Pallas kernels, reduce_grads(): pl.pallas_call(reduce_kernel, out_shape=jax.ShapeDtypeStruct((64, 128), f...  35.7 us
    pallas_call x1, Pallas kernels, exchange_stats(): pl.pallas_call(stats_kernel, out_shape=jax.ShapeDtypeStruct((2,) + shape,...  26 us
    pallas_call x1, Pallas kernels, gather_grads(): pl.pallas_call(gather_kernel, out_shape=jax.ShapeDtypeStruct((2 * part.sh...  22 us
    dot_general x1, matrix products, body(): lax.dot_general(x_ref, g_ref, contract_last, preferred_element_type=f32)  5.12 us

profile of v1, /device:TPU:1, one launch (start us, length us, event | category | flops | bytes accessed | tf_op | source)
XLA Modules:
  0.0 231.2 jit_solution(8514781407928577461)
XLA Ops:
  0.7 0.7 scatter.6
  1.3 0.8 scatter.9.meta
  2.1 0.0 copy-start.1
  2.1 0.6 copy-done.1
  2.7 121.0 %spread.1 = (bf16[640,4096]{1,0:T(8,128)(2,1)}, bf16[640,4096]{1,0:T(8,128)(2,1)}, bf16[256,4096]{1,0:T(8,128)(2,1)}, bf16[256,4096]{1,0:T(8,128)(2,1)}, s32[8,8,256]{2,1,0:T(8,128)}) custom-call(bf16[160,4096]{1,0:T(8,128)(2,1)} %hid_ref.1, bf16[160,4096]{1,0:T(8,128)(2,1)} %hid_train.1, bf16[1008,512]{1,0:T(8,128)(2,1)} %head_ref.1, ...), custom_call_target="tpu_custom_call" | custom-call | tf_op jit(solution)/shard_map/spread/pallas_call | solution.py:284
  123.7 0.9 fusion.21
  124.7 1.2 reduce-window.15
  125.9 0.1 slice.110
  126.0 0.1 copy.19
  126.1 0.1 copy.20
  126.2 0.1 add_bitcast_fusion
  126.4 0.1 eq.47
  126.5 0.0 copy-start.3
  126.5 5.1 %fusion.22 = f32[640,256]{0,1:T(8,128)S(1)} fusion(bf16[640,4096]{1,0:T(8,128)(2,1)} %get-tuple-element.32, bf16[256,4096]{1,0:T(8,128)(2,1)} %get-tuple-element.33), kind=kOutput, calls=%fused_computation.58 | convolution fusion | flops 1342177280 | bytes 7995392 | tf_op jit(solution)/shard_map/dot_general | solution.py:586
  131.6 0.0 copy-done.3
  131.6 4.3 %select_reduce_fusion.2 = (f32[640]{0:T(1024)S(1)}, f32[640]{0:T(1024)S(1)}, f32[640,256]{0,1:T(8,128)S(1)}) fusion(pred[256]{0:T(512)(128)(4,1)S(1)} %compare_or_fusion, f32[640,256]{0,1:T(8,128)S(1)} %fusion.22, bf16[640,4096]{1,0:T(8,128)(2,1)} %get-tuple-element.35, bf16[256,4096]{1,0:T(8,128)(2,1)S(1)} %copy-done.3), kind=kOutput, calls=%fused_computation.8 | convolution fusion | flops 1342831360 | bytes 8656128 | tf_op jit(solution)/shard_map/dot_general | solution.py:585
  135.9 0.5 select_reduce_fusion
  136.5 0.6 stack.31.mine
  137.2 26.0 %stats.1 = f32[2,8,640]{2,1,0:T(8,128)} custom-call(f32[8,640]{1,0:T(8,128)} %stack.31.mine), custom_call_target="tpu_custom_call" | custom-call | tf_op jit(solution)/shard_map/stats/pallas_call | solution.py:365
  163.1 0.8 dynamic-slice_reduce_fusion.2
  164.0 0.3 select_convert_fusion
  164.3 0.2 copy.22
  164.4 1.2 convolution_convert_fusion
  165.7 22.0 %gather_grads.1 = bf16[896,1024]{1,0:T(8,128)(2,1)} custom-call(bf16[448,256]{1,0:T(8,128)(2,1)} %bitcast.37), custom_call_target="tpu_custom_call" | custom-call | tf_op jit(solution)/shard_map/gather_grads/pallas_call | solution.py:443
  187.6 0.0 slice-start
  187.6 0.0 slice-start.1
  187.7 1.8 pad.19
  189.5 0.0 slice-done
  189.5 0.0 slice-done.1
  189.5 1.3 fusion.grad
  190.8 0.0 copy-start.2
  190.8 0.0 copy-start
  190.8 35.7 %reduce_grads.1 = f32[64,128]{1,0:T(8,128)S(1)} custom-call(f32[512,1024]{1,0:T(8,128)S(1)} %fusion.grad), custom_call_target="tpu_custom_call" | custom-call | tf_op jit(solution)/shard_map/reduce_grads/pallas_call | solution.py:549
  226.5 0.0 copy-done.2
  226.5 0.3 reduce-window.19
  226.9 0.1 slice.107
  227.0 0.1 slice_reduce_fusion
  227.1 0.1 add_bitcast_fusion.1
  227.2 0.8 fusion.9
  228.0 0.0 copy-done
  228.0 0.1 subtract_reduce_fusion.1
  228.1 0.1 sub.81
  228.1 0.6 fusion.13
  229.4 0.1 sub.83
  229.5 0.6 fusion.14
  (23 shorter events, 0.2 us)
Async XLA Ops:
  2.1 0.6 copy-start.1
  126.5 5.1 %copy-start.3 = (bf16[256,4096]{1,0:T(8,128)(2,1)S(1)}, bf16[256,4096]{1,0:T(8,128)(2,1)}, u32[]{:S(2)}) copy-start(bf16[256,4096]{1,0:T(8,128)(2,1)} %get-tuple-element.36) | copy-start | bytes 6291460
  187.6 1.9 slice-start
  187.6 1.9 slice-start.1
  190.8 35.7 %copy-start.2 = (s32[160]{0:T(256)S(1)}, s32[160]{0:T(256)}, u32[]{:S(2)}) copy-start(s32[160]{0:T(256)} %param.15) | copy-start | bytes 1924
  190.8 37.2 %copy-start = (f32[2,8,640]{2,1,0:T(8,128)S(1)}, f32[2,8,640]{2,1,0:T(8,128)}, u32[]{:S(2)}) copy-start(f32[2,8,640]{2,1,0:T(8,128)} %stats.1) | copy-start | bytes 122884

commit v2 on v0

v2 whole, which is shorter than its diff:
```python
import functools

import jax
import jax.numpy as jnp
from jax import lax
from jax.experimental import pallas as pl
from jax.experimental.pallas import tpu as pltpu
from jax.sharding import PartitionSpec as P

MESH = pl.DeviceIdType.MESH
NX, NY, NZ = 4, 8, 8
loss_scale = 64.0
TOK = 160
SEL = 100
SLOT = 112
ROWS = 128
PIECE = 128
FEAT = 512
WIDTH = 4096
HALF = 4 * SLOT
LANES = 256
FAR_FIRST = (4, 3, 5, 2, 6, 1, 7)
NEAR_FIRST = (1, 7, 2, 6, 3, 5, 4)
LAST = (((1,), (1,)), ((), ()))
REF, TRAIN = 0, 1


def coords():
    z = lax.axis_index("dp")
    v = lax.axis_index("vocab")
    return v // 16, (v // 2) % NY, z, v % 2


def vocab_index(x, y, c):
    return (x * NY + y) * 2 + c


def remote(src, dst, send_sem, recv_sem, device):
    return pltpu.make_async_remote_copy(
        src_ref=src, dst_ref=dst, send_sem=send_sem, recv_sem=recv_sem,
        device_id=device, device_id_type=MESH,
    )


def aligned(start, size, step):
    return pl.ds(pl.multiple_of(start, step), size)


def kernel(
    hid_ref, hid_train, head_ref, head_train, meta,
    piece_out, stats_out, meta_all,
    xbuf, gbuf, home, logits, stats, zstat, xstat, ystat,
    chosen, gathered, grad, cgrad, acc, xgrad, turned, ygrad, summed,
    local_sem, z_send, z_recv, m_send, m_recv, w_send, w_recv, s_send, s_recv,
    rx_send, rx_recv, ry_send, ry_recv,
    tz_send, tz_recv, tx_send, tx_recv, ty_send, ty_recv, tc_send, tc_recv,
    ec_send, ec_recv, ez_send, ez_recv,
    gc_send, gc_recv, gx_send, gx_recv, gy_send, gy_recv, f_send, f_recv,
):
    f32 = jnp.float32
    x, y, z, c = coords()
    v = vocab_index(x, y, c)
    sibling = (z, vocab_index(x, y, 1 - c))
    z_peers = [None] + [((z + s) % NZ, v) for s in range(1, NZ)]
    x_peers = [None] + [(z, vocab_index((x + s) % NX, y, c)) for s in range(1, NX)]
    y_peers = [None] + [(z, vocab_index(x, (y + s) % NY, c)) for s in range(1, NY)]
    dest = (4 * c + y // 2, 8 * z + 2 * x + y % 2)
    j = v % 8
    origin = (v // 8, vocab_index(j // 2, (z % 4) * 2 + j % 2, z // 4))
    stays = jnp.logical_and(dest[0] == z, dest[1] == v)
    leaves = jnp.logical_not(stays)

    barrier = pltpu.get_barrier_semaphore()
    friends = z_peers[1:] + x_peers[1:] + y_peers[1:] + [sibling]
    for device in friends:
        pl.semaphore_signal(barrier, inc=1, device_id=device, device_id_type=MESH)

    @pl.when(leaves)
    def _():
        for device in (dest, origin):
            pl.semaphore_signal(barrier, inc=1, device_id=device, device_id_type=MESH)

    pl.semaphore_wait(barrier, len(friends) + 2 - 2 * stays.astype(jnp.int32))

    is_source = z // 4 == c
    hid = (hid_ref, hid_train)
    heads = (head_ref, head_train)

    def when_active(r, act):
        if r:
            act()
        else:
            pl.when(jnp.logical_not(is_source))(act)

    def own_piece(r):
        if r < 2:
            return aligned((y * NX + x) * PIECE, PIECE, PIECE)
        return aligned((x * NY + y) * PIECE, PIECE, PIECE)

    def z_copy(a, s):
        columns = own_piece(-s % 4)
        return remote(
            hid[a].at[:, columns], xbuf.at[a, aligned(TOK * (z % 4), TOK, 16), columns],
            z_send.at[a, s - 1], z_recv.at[a, -s % 4], z_peers[s],
        )

    def z_arrival(a, r):
        columns = own_piece(r)
        part = xbuf.at[a, aligned(TOK * ((z + r) % 4), TOK, 16), columns]
        return remote(part, part, z_send.at[a, 0], z_recv.at[a, r], sibling)

    def own_tokens(a):
        return pltpu.make_async_copy(
            hid[a], xbuf.at[a, aligned(TOK * (z % 4), TOK, 16), :], local_sem.at[a]
        )

    def meta_copy(s, arriving):
        source = (z + NZ - s) % NZ if arriving else z
        return remote(meta, meta_all.at[source], m_send.at[s - 1], m_recv.at[s - 1], z_peers[s])

    def row_block(q):
        return aligned(q * ROWS - 16 * (q // 7), ROWS, 16)

    def head_part(a, core, source):
        return gbuf.at[a, aligned(ROWS * core, ROWS, ROWS), aligned(source * FEAT, FEAT, FEAT)]

    def head_copy(a, s, arriving):
        source = (z + NZ - s) % NZ if arriving else z
        return remote(
            heads[a].at[row_block((z + s) % NZ), :], head_part(a, c, source),
            w_send.at[a, s - 1], w_recv.at[a, s - 1], z_peers[s],
        )

    def own_rows(a):
        return pltpu.make_async_copy(
            heads[a].at[row_block(z), :], head_part(a, c, z), local_sem.at[2 + a]
        )

    def share_copy(a, s, arriving):
        part = head_part(a, 1 - c if arriving else c, (z + NZ - s) % NZ)
        return remote(part, part, s_send.at[a, s], s_recv.at[a, s], sibling)

    own_meta = pltpu.make_async_copy(meta, meta_all.at[z], local_sem.at[4])
    home_copies = [
        pltpu.make_async_copy(
            head_train.at[pl.ds(0, 7 * ROWS), :], home.at[pl.ds(0, 7 * ROWS), :], local_sem.at[5]
        ),
        pltpu.make_async_copy(
            head_train.at[pl.ds(7 * ROWS - 16, ROWS), :], home.at[pl.ds(7 * ROWS, ROWS), :],
            local_sem.at[6],
        ),
    ]

    def ring_copy(a, r, axis, step, way, arriving):
        size, pos, peers = (NX, x, x_peers) if axis == "x" else (NY, y, y_peers)
        send, recv = (rx_send, rx_recv) if axis == "x" else (ry_send, ry_recv)
        back = step if arriving else step - 1
        sign = -1 if way == 0 else 1
        block = (pos + sign * back + size) % size
        group = NX * PIECE if r < 2 else NY * PIECE
        if (axis == "x") == (r < 2):
            base = y if r < 2 else x
            columns = aligned(base * group + block * PIECE, PIECE, PIECE)
        else:
            columns = aligned(block * group, group, group)
        start = TOK * ((z + r) % 4)
        if 2 * step == size:
            rows = aligned(start + way * (TOK // 2), TOK // 2, 16)
        else:
            rows = aligned(start, TOK, 16)
        part = xbuf.at[a, rows, columns]
        index = (a, r, step - 1, way)
        return remote(part, part, send.at[index], recv.at[index], peers[1 if way == 0 else size - 1])

    def ring_send(a, r, axis, step):
        for way in (0, 1):
            ring_copy(a, r, axis, step, way, False).start()

    def ring_wait(a, r, axis, step):
        for way in (0, 1):
            ring_copy(a, r, axis, step, way, True).wait_recv()

    def advance(a, *moves):
        for group, axis, step, next_axis, next_step in moves:
            for r in group:
                def act(r=r):
                    ring_wait(a, r, axis, step)
                    if next_axis:
                        ring_send(a, r, next_axis, next_step)
                when_active(r, act)

    A, B = (1, 0), (2, 3)

    def start_rings(a):
        for r in (2, 3, 1, 0):
            def act(r=r):
                z_arrival(a, r).wait_recv()
                ring_send(a, r, "x" if r < 2 else "y", 1)
            when_active(r, act)

    def pass_heads(a, distances):
        for s in distances:
            head_copy(a, s, True).wait_recv()
            share_copy(a, s, False).start()

    for a in (TRAIN, REF):
        @pl.when(is_source)
        def _():
            for s in FAR_FIRST:
                z_copy(a, s).start()
            own_tokens(a).start()
        if a == TRAIN:
            own_meta.start()
            for s in range(1, NZ):
                meta_copy(s, False).start()
        own_rows(a).start()
        for s in FAR_FIRST:
            head_copy(a, s, False).start()
    for copy in home_copies:
        copy.start()
    zero_stats = jnp.zeros((16, LANES), f32)
    for a in (REF, TRAIN):
        stats[a, 0] = zero_stats

    start_rings(TRAIN)
    advance(TRAIN, (B, "y", 1, "y", 2), (A, "x", 1, "x", 2))
    advance(TRAIN, (B, "y", 2, "y", 3), (A, "x", 2, "y", 1))
    advance(TRAIN, (B, "y", 3, "y", 4))
    advance(TRAIN, (B, "y", 4, "x", 1))
    own_rows(TRAIN).wait()
    share_copy(TRAIN, 0, False).start()
    advance(TRAIN, (A, "y", 1, "y", 2))
    start_rings(REF)
    advance(TRAIN, (A, "y", 2, "y", 3))
    pass_heads(TRAIN, (1, 7, 2, 6))
    advance(TRAIN, (B, "x", 1, "x", 2))
    advance(REF, (B, "y", 1, "y", 2), (A, "x", 1, "x", 2))
    advance(TRAIN, (A, "y", 3, "y", 4))
    advance(REF, (B, "y", 2, "y", 3), (A, "x", 2, "y", 1))
    pass_heads(TRAIN, (3, 5, 4))
    advance(REF, (B, "y", 3, "y", 4))
    advance(REF, (B, "y", 4, "x", 1))
    advance(TRAIN, (A, "y", 4, None, 0), (B, "x", 2, None, 0))
    own_meta.wait()
    for s in range(1, NZ):
        meta_copy(s, True).wait_recv()
    for s in range(NZ):
        share_copy(TRAIN, s, True).wait_recv()

    @pl.when(is_source)
    def _():
        own_tokens(TRAIN).wait()

    row = lax.broadcasted_iota(jnp.int32, (2 * ROWS, TOK), 0)
    within = row % ROWS
    chip = v // 2
    row_id = (2 * chip + row // ROWS) * 1008 + z * ROWS - 16 * (z // 7) + within
    valid = jnp.logical_or(within >= 16, z < 7)

    def hits(i):
        return jnp.logical_and(row_id == meta_all[4 * c + i][0:1, :TOK], valid)

    def local_stats(a):
        for i in range(4):
            table = lax.dot_general(
                gbuf[a], xbuf[a, TOK * i:TOK * (i + 1), :], LAST, preferred_element_type=f32
            )
            if a == TRAIN:
                logits[i] = table
            top = jnp.max(jnp.where(valid, table, -jnp.inf), axis=0, keepdims=True)
            parts = jnp.where(valid, jnp.exp(table - top), 0.0)
            picked = jnp.where(hits(i), table, 0.0)
            stats[a, 0, i:i + 1, :TOK] = top
            stats[a, 0, 4 + i:5 + i, :TOK] = jnp.sum(parts, axis=0, keepdims=True)
            stats[a, 0, 8 + i:9 + i, :TOK] = jnp.sum(picked, axis=0, keepdims=True)

    levels = (
        (z_peers, zstat, tz_send, tz_recv),
        (x_peers, xstat, tx_send, tx_recv),
        (y_peers, ystat, ty_send, ty_recv),
    )

    def stat_copies(a, level):
        peers, buf, send, recv = levels[level]
        return [
            remote(stats.at[a, level], buf.at[a, s], send.at[a, s], recv.at[a, s], peers[s + 1])
            for s in range(len(peers) - 1)
        ]

    def stat_send(a, level):
        for copy in stat_copies(a, level):
            copy.start()

    def stat_merge(a, level):
        copies = stat_copies(a, level)
        for copy in copies:
            copy.wait_recv()
        blocks = [stats[a, level]] + [levels[level][1][a, s] for s in range(len(copies))]
        top = functools.reduce(jnp.maximum, [b[0:4] for b in blocks])
        total = sum(b[4:8] * jnp.exp(b[0:4] - top) for b in blocks)
        picked = sum(b[8:12] for b in blocks)
        merged = jnp.concatenate([top, total, picked, jnp.zeros_like(top)], axis=0)
        if level < 2:
            stats[a, level + 1] = merged
        else:
            stats_out[a, c] = merged

    def stat_share(a, arriving):
        part = stats_out.at[a, 1 - c if arriving else c]
        return remote(part, part, tc_send.at[a], tc_recv.at[a], sibling)

    local_stats(TRAIN)
    stat_send(TRAIN, 0)
    advance(REF, (A, "y", 1, "y", 2))
    stat_merge(TRAIN, 0)
    stat_send(TRAIN, 1)
    advance(REF, (A, "y", 2, "y", 3))
    stat_merge(TRAIN, 1)
    stat_send(TRAIN, 2)
    own_rows(REF).wait()
    share_copy(REF, 0, False).start()
    stat_merge(TRAIN, 2)
    stat_share(TRAIN, False).start()

    upper = (
        lax.broadcasted_iota(jnp.int32, (TOK, TOK), 0)
        <= lax.broadcasted_iota(jnp.int32, (TOK, TOK), 1)
    ).astype(jnp.bfloat16)
    place = lax.broadcasted_iota(jnp.int32, (SLOT, TOK), 0)
    for i in range(4):
        weight = meta_all[4 * c + i][1:2, :TOK]
        count = jnp.dot(
            jnp.broadcast_to(weight, (8, TOK)).astype(jnp.bfloat16), upper,
            preferred_element_type=f32,
        )[0:1].astype(jnp.int32)
        pick = jnp.logical_and(place == count - 1, weight != 0).astype(jnp.bfloat16)
        top = stats_out[TRAIN, c][i:i + 1, :TOK]
        total = stats_out[TRAIN, c][4 + i:5 + i, :TOK]
        share = jnp.exp(logits[i] - top) / total
        slope = jnp.where(valid, loss_scale * (share - hits(i).astype(f32)), 0.0)
        rows = lax.dot_general(
            pick, slope.astype(jnp.bfloat16), LAST, preferred_element_type=f32
        ).astype(jnp.bfloat16)
        for k in (0, 1):
            chosen[k, SLOT * i:SLOT * (i + 1), :] = rows[:, ROWS * k:ROWS * (k + 1)]

    def half_rows(h):
        return aligned(h * HALF, HALF, 16)

    own_chosen = pltpu.make_async_copy(
        chosen.at[c], gathered.at[z, half_rows(c), :], local_sem.at[7]
    )
    chosen_share = remote(
        chosen.at[1 - c], gathered.at[z, half_rows(c), :], ec_send, ec_recv, sibling
    )
    chosen_arrival = remote(
        chosen.at[c], gathered.at[z, half_rows(1 - c), :], ec_send, ec_recv, sibling
    )

    def e_copy(step, way, index, arriving):
        h = c if index == 0 else 1 - c
        back = step if arriving else step - 1
        sign = -1 if way == 0 else 1
        part = gathered.at[(z + sign * back + NZ) % NZ, half_rows(h), :]
        src = chosen.at[c] if step == 1 and index == 0 and not arriving else part
        return remote(
            src, part, ez_send.at[step - 1, way, index], ez_recv.at[step - 1, way, index],
            z_peers[1 if way == 0 else NZ - 1],
        )

    def e_advance(step):
        for index in (0, 1):
            for way in (0, 1):
                if step < 4 or way == index:
                    e_copy(step, way, index, True).wait_recv()
                if step < 3 or (step == 3 and way == index):
                    e_copy(step + 1, way, index, False).start()

    chosen_share.start()
    for way in (0, 1):
        e_copy(1, way, 0, False).start()
    own_chosen.start()
    chosen_arrival.wait_recv()
    for way in (0, 1):
        e_copy(1, way, 1, False).start()
    advance(REF, (A, "y", 3, "y", 4), (B, "x", 1, "x", 2))
    e_advance(1)
    pass_heads(REF, (1, 7))
    e_advance(2)
    pass_heads(REF, (2, 6))
    e_advance(3)
    pass_heads(REF, (3, 5, 4))
    advance(REF, (A, "y", 4, None, 0), (B, "x", 2, None, 0))
    for s in range(NZ):
        share_copy(REF, s, True).wait_recv()

    @pl.when(is_source)
    def _():
        own_tokens(REF).wait()

    local_stats(REF)
    stat_send(REF, 0)
    e_advance(4)
    own_chosen.wait()
    for copy in home_copies:
        copy.wait()

    for d in range(NZ):
        columns = jnp.concatenate(
            [gathered[q, SLOT * d:SLOT * (d + 1), :] for q in range(NZ)], axis=1
        )
        table = jnp.dot(columns, home[...], preferred_element_type=f32)
        for q in range(NX):
            grad[q, SLOT * d:SLOT * (d + 1), :] = table[:, 128 * q:128 * (q + 1)]

    def grad_share(q):
        return remote(
            grad.at[q, aligned(HALF * (1 - c), HALF, 16), :], cgrad.at[q],
            gc_send.at[q], gc_recv.at[q], sibling,
        )

    def x_copy(s):
        return remote(
            acc.at[(x + s) % NX], xgrad.at[s - 1], gx_send.at[s - 1], gx_recv.at[s - 1], x_peers[s]
        )

    def y_copy(s):
        q = (y + s) % NY
        return remote(
            turned.at[q // 2, aligned((q % 2) * 64, 64, 64), :], ygrad.at[s - 1],
            gy_send.at[s - 1], gy_recv.at[s - 1], y_peers[s],
        )

    order = (2, 1, 3, 0)
    for s in order:
        grad_share((x + s) % NX).start()
    for s in order:
        q = (x + s) % NX
        grad_share(q).wait_recv()
        acc[q] = grad[q, aligned(HALF * c, HALF, 16), :] + cgrad[q]
        if s:
            x_copy(s).start()
    stat_merge(REF, 0)
    stat_send(REF, 1)
    for s in range(1, NX):
        x_copy(s).wait_recv()
    total = acc[x] + xgrad[0] + xgrad[1] + xgrad[2]
    for i in range(4):
        block = jnp.concatenate(
            [total[SLOT * i:SLOT * (i + 1)], jnp.zeros((128 - SLOT, 128), f32)], axis=0
        )
        turned[i] = block.T
    for s in FAR_FIRST:
        y_copy(s).start()
    stat_merge(REF, 1)
    stat_send(REF, 2)
    for s in range(1, NY):
        y_copy(s).wait_recv()
    summed[...] = turned[y // 2, aligned((y % 2) * 64, 64, 64), :] + sum(
        ygrad[s] for s in range(NY - 1)
    )
    final = remote(summed, piece_out, f_send, f_recv, dest)
    stay = pltpu.make_async_copy(summed, piece_out, local_sem.at[8])

    @pl.when(leaves)
    def _():
        final.start()

    @pl.when(stays)
    def _():
        stay.start()

    stat_merge(REF, 2)
    stat_share(REF, False).start()
    for a in (TRAIN, REF):
        stat_share(a, True).wait_recv()

    @pl.when(leaves)
    def _():
        final.wait_recv()
        final.wait_send()

    @pl.when(stays)
    def _():
        stay.wait()

    for a in (REF, TRAIN):
        @pl.when(is_source)
        def _():
            for s in range(1, NZ):
                z_copy(a, s).wait_send()
        for s in range(1, NZ):
            head_copy(a, s, False).wait_send()
        for s in range(NZ):
            share_copy(a, s, False).wait_send()
        for level in range(3):
            for copy in stat_copies(a, level):
                copy.wait_send()
        stat_share(a, False).wait_send()
        for r in range(4):
            def act(r=r):
                for axis, size in (("x", NX), ("y", NY)):
                    for step in range(1, size // 2 + 1):
                        for way in (0, 1):
                            ring_copy(a, r, axis, step, way, False).wait_send()
            when_active(r, act)
    for s in range(1, NZ):
        meta_copy(s, False).wait_send()
    chosen_share.wait_send()
    for step in (1, 2, 3, 4):
        for index in (0, 1):
            for way in (0, 1):
                if step < 4 or way == index:
                    e_copy(step, way, index, False).wait_send()
    for q in range(NX):
        grad_share(q).wait_send()
    for s in range(1, NX):
        x_copy(s).wait_send()
    for s in range(1, NY):
        y_copy(s).wait_send()


def fused(hidden_ref, hidden_train, head_ref, head_train, meta):
    anywhere = pl.BlockSpec(memory_space=pl.ANY)
    vmem = pl.BlockSpec(memory_space=pltpu.VMEM)
    dma = pltpu.SemaphoreType.DMA
    sds = jax.ShapeDtypeStruct
    f32, bf16 = jnp.float32, jnp.bfloat16
    buf = pltpu.VMEM
    pairs = [
        (2, NZ - 1), (2, 4), (NZ - 1,), (NZ - 1,), (2, NZ - 1), (2, NZ - 1), (2, NZ), (2, NZ),
        (2, 4, 2, 2), (2, 4, 2, 2), (2, 4, 4, 2), (2, 4, 4, 2),
        (2, NZ - 1), (2, NZ - 1), (2, NX - 1), (2, NX - 1), (2, NY - 1), (2, NY - 1), (2,), (2,),
    ]
    return pl.pallas_call(
        kernel,
        out_shape=[
            sds((64, 128), f32), sds((2, 2, 16, LANES), f32), sds((NZ,) + meta.shape, meta.dtype),
        ],
        in_specs=[anywhere] * 5,
        out_specs=[vmem] * 3,
        scratch_shapes=[
            buf((2, 4 * TOK, WIDTH), bf16), buf((2, 2 * ROWS, WIDTH), bf16),
            buf((NZ * ROWS, FEAT), bf16), buf((4, 2 * ROWS, TOK), f32),
            buf((2, 3, 16, LANES), f32), buf((2, NZ - 1, 16, LANES), f32),
            buf((2, NX - 1, 16, LANES), f32), buf((2, NY - 1, 16, LANES), f32),
            buf((2, HALF, ROWS), bf16), buf((NZ, 2 * HALF, ROWS), bf16),
            buf((NX, 2 * HALF, 128), f32), buf((NX, HALF, 128), f32), buf((NX, HALF, 128), f32),
            buf((NX - 1, HALF, 128), f32), buf((4, 128, 128), f32),
            buf((NY - 1, 64, 128), f32), buf((64, 128), f32),
            dma((9,)), *[dma(shape) for shape in pairs],
            dma, dma, dma((4, 2, 2)), dma((4, 2, 2)),
            dma((NX,)), dma((NX,)), dma((NX - 1,)), dma((NX - 1,)),
            dma((NY - 1,)), dma((NY - 1,)), dma, dma,
        ],
        compiler_params=pltpu.CompilerParams(
            collective_id=0, has_side_effects=True, vmem_limit_bytes=60 * 1024 * 1024
        ),
        name="fused",
    )(hidden_ref, hidden_train, head_ref, head_train, meta)


def body(hidden_ref, hidden_train, head_ref, head_train, targets, mask):
    f32 = jnp.float32
    x, y, z, c = coords()
    meta = jnp.pad(jnp.stack([targets, mask]), ((0, 6), (0, LANES - TOK)))
    piece, both, meta_all = fused(hidden_ref, hidden_train, head_ref, head_train, meta)

    both = both[:, :, :12, :TOK].reshape(2, 2, 3, 4, TOK)
    cross = jnp.log(both[:, :, 1]) + both[:, :, 0] - both[:, :, 2]
    cross = cross.reshape(2, NZ, TOK)
    excess_all = cross[TRAIN] - cross[REF]
    excess = lax.dynamic_slice_in_dim(excess_all, z, 1, 0).reshape(TOK)
    weight_all = meta_all[:, 1, :TOK].astype(f32)
    loss_value = jnp.sum(weight_all * cross[TRAIN]) / (NZ * SEL)

    upper = jnp.triu(jnp.ones((TOK, TOK), f32))
    count = jnp.dot(mask.astype(f32)[None, :], upper)
    place = jnp.logical_and(
        jnp.arange(128, dtype=f32)[:, None] == count - 1.0, mask[None, :] != 0
    ).astype(f32)
    hidden_grad = lax.dot_general(
        piece, place, (((1,), (0,)), ((), ())), precision=lax.Precision.HIGHEST,
        preferred_element_type=f32,
    )
    return (excess, loss_value, hidden_grad)


def solution(mesh):
    in_specs = (P("dp", None), P("dp", None), P("vocab", "dp"), P("vocab", "dp"), P("dp"), P("dp"))
    out_specs = (P("dp"), P(), P("vocab", "dp"))
    return jax.shard_map(body, mesh=mesh, in_specs=in_specs, out_specs=out_specs, check_vma=False)
```

time: 626 us -> 168 us (0.27)
  waiting for transfers between devices: 312 us -> 0 us
  blocking collectives: 265 us -> 0 us
  Pallas kernels: 0 us -> 157 us
  matrix products: 17.5 us -> 1.8 us
  between operations: 15.6 us -> 2.46 us
    all_gather x2 -> x0, waiting for transfers between devices: 190 us -> none  [the longest x1 99.4 us: body(): lax.all_gather(head_ref, 'dp', axis=1, tiled=True)]
    pallas_call x0 -> x1, Pallas kernels: none -> 157 us  [fused(): pl.pallas_call(kernel, out_shape=[sds((64, 128), f32), sds((2, 2, 16, LAN...]
    psum x2 -> x0, blocking collectives: 141 us -> none  [the longest x1 128 us: body(): lax.psum((jnp.sum(jnp.exp(ref_logits - ref_max[:, None]), axis=1), jnp.su...]
    pmax x1 -> x0, blocking collectives: 124 us -> none  [body(): ref_max, train_max = lax.pmax((local_ref_max, local_train_max), 'vocab')]
    unnamed x4 -> x0, waiting for transfers between devices: 123 us -> none
    dot_general x3 -> x2, matrix products: 17.5 us -> 1.8 us  [the longest x1 1.6 us: body(): lax.dot_general(piece, place, (((1,), (0,)), ((), ())), precision=lax.Pre...]
  transfers between devices with their start and end apart: 3 -> 0, of which waited for: 3 -> 0; matrix products, arithmetic and copies ran while one was open for 2% -> 0% of each run, Pallas kernels for 0% -> 0%
where the time goes in v2:
time: 168 us; the launch traced here: 165 us
  Pallas kernels  157 us (93%)
  between operations  2.46 us (1%)
  other arithmetic  2.2 us (1%)
  local copies, waits for them, and re-layouts  2.07 us (1%)
  matrix products  1.8 us (1%)
    pallas_call x1, Pallas kernels, fused(): pl.pallas_call(kernel, out_shape=[sds((64, 128), f32), sds((2, 2, 16, LAN...  157 us

profile of v2, /device:TPU:1, one launch (start us, length us, event | category | flops | bytes accessed | tf_op | source)
XLA Modules:
  0.0 165.0 jit_solution(10499791235400933926)
XLA Ops:
  0.6 0.7 pad_add_fusion
  1.3 0.6 pad.4.meta
  1.9 0.0 copy-start
  1.9 156.5 %fused.1 = (f32[64,128]{1,0:T(8,128)}, f32[2,2,16,256]{3,2,1,0:T(8,128)}, s32[8,8,256]{2,1,0:T(8,128)}) custom-call(bf16[160,4096]{1,0:T(8,128)(2,1)} %hid_ref.1, bf16[160,4096]{1,0:T(8,128)(2,1)} %hid_train.1, bf16[1008,512]{1,0:T(8,128)(2,1)} %head_ref.1, bf16[1008,512]{1,0:T(8,128)(2,1)} %head_train.1, s32[8,256]{1,0:T(8,128)} %pad.4.meta), custom_call_target="tpu_custom_call" | custom-call | tf_op jit(solution)/shard_map/fused/pallas_call | solution.py:535
  158.5 0.8 slice_convert_fusion
  159.3 0.9 copy.14
  160.2 0.6 fusion.11
  160.8 0.6 constant_dynamic-slice_fusion
  162.1 0.0 copy-done
  162.1 0.2 fusion
  162.3 1.6 fusion.3
  (7 shorter events, 0.1 us)
Async XLA Ops:
  1.9 160.1 %copy-start = (s32[160]{0:T(256)S(1)}, s32[160]{0:T(256)}, u32[]{:S(2)}) copy-start(s32[160]{0:T(256)} %param.11) | copy-start | bytes 1924

commit v3 on v0

v3 whole, which is shorter than its diff:
```python
import functools

import jax
import jax.numpy as jnp
from jax import lax
from jax.experimental import pallas as pl
from jax.experimental.pallas import tpu as pltpu
from jax.sharding import PartitionSpec as P

MESH = pl.DeviceIdType.MESH
NX, NY, NZ = 4, 8, 8
loss_scale = 64.0
TOK = 160
SEL = 100
SLOT = 112
ROWS = 128
PIECE = 128
FEAT = 512
WIDTH = 4096
PAIR = 2 * SLOT
LANES = 256
BOTH = 2 * ROWS
FAR_FIRST = (4, 3, 5, 2, 6, 1, 7)
LAST = (((1,), (1,)), ((), ()))
REF, TRAIN = 0, 1


def coords():
    z = lax.axis_index("dp")
    v = lax.axis_index("vocab")
    return v // 16, (v // 2) % NY, z, v % 2


def vocab_index(x, y, c):
    return (x * NY + y) * 2 + c


def remote(src, dst, send_sem, recv_sem, device):
    return pltpu.make_async_remote_copy(
        src_ref=src, dst_ref=dst, send_sem=send_sem, recv_sem=recv_sem,
        device_id=device, device_id_type=MESH,
    )


def aligned(start, size, step):
    return pl.ds(pl.multiple_of(start, step), size)


def kernel(
    hid_ref, hid_train, head_ref, head_train, meta,
    grad_out, excess_out, loss_out,
    meta_all, both, xbuf, gbuf, home, logits, stats, zstat, xstat, ystat,
    gathered, grad, xgrad, turned, ygrad, summed, piece,
    local_sem, z_send, z_recv, m_send, m_recv, w_send, w_recv, s_send, s_recv,
    h_local, h_send, h_recv, ay_send, ay_recv, by_send, by_recv, bx_send, bx_recv,
    tz_send, tz_recv, tx_send, tx_recv, ty_send, ty_recv, tc_send, tc_recv,
    ez_send, ez_recv, gx_send, gx_recv, gy_send, gy_recv, f_send, f_recv,
):
    f32 = jnp.float32
    x, y, z, c = coords()
    v = vocab_index(x, y, c)
    sibling = (z, vocab_index(x, y, 1 - c))
    z_peers = [None] + [((z + s) % NZ, v) for s in range(1, NZ)]
    x_peers = [None] + [(z, vocab_index((x + s) % NX, y, c)) for s in range(1, NX)]
    y_peers = [None] + [(z, vocab_index(x, (y + s) % NY, c)) for s in range(1, NY)]
    dests = [(4 * c + 2 * b + y // 4, 8 * z + 2 * x + (y % 4) // 2) for b in (0, 1)]
    origins = [
        (v // 8, vocab_index((v % 8) // 2, 4 * (z % 2) + 2 * (v % 2) + h, z // 4)) for h in (0, 1)
    ]

    def is_here(device):
        return jnp.logical_and(device[0] == z, device[1] == v)

    barrier = pltpu.get_barrier_semaphore()
    friends = z_peers[1:] + x_peers[1:] + y_peers[1:] + [sibling]
    for device in friends:
        pl.semaphore_signal(barrier, inc=1, device_id=device, device_id_type=MESH)
    expected = len(friends) + 4
    for device in dests + origins:
        expected = expected - is_here(device).astype(jnp.int32)

        @pl.when(jnp.logical_not(is_here(device)))
        def _():
            pl.semaphore_signal(barrier, inc=1, device_id=device, device_id_type=MESH)

    pl.semaphore_wait(barrier, expected)

    is_source = z // 4 == c
    hid = (hid_ref, hid_train)
    heads = (head_ref, head_train)

    def when_active(r, act):
        if r:
            act()
        else:
            pl.when(jnp.logical_not(is_source))(act)

    def z_columns(r):
        if r < 2:
            return aligned(y * FEAT, FEAT, FEAT)
        return aligned((x * NY + y) * PIECE, PIECE, PIECE)

    def z_copy(a, s):
        r = -s % 4
        columns = z_columns(r)
        return remote(
            hid[a].at[:, columns], xbuf.at[a, pl.ds(TOK * r, TOK), columns],
            z_send.at[a, s - 1], z_recv.at[a, r], z_peers[s],
        )

    def z_arrival(a, r):
        part = xbuf.at[a, pl.ds(TOK * r, TOK), z_columns(r)]
        return remote(part, part, z_send.at[a, 0], z_recv.at[a, r], sibling)

    def own_tokens(a):
        return pltpu.make_async_copy(hid[a], xbuf.at[a, pl.ds(0, TOK), :], local_sem.at[a])

    def meta_copy(s, arriving):
        source = (z + NZ - s) % NZ if arriving else z
        return remote(meta, meta_all.at[source], m_send.at[s - 1], m_recv.at[s - 1], z_peers[s])

    def row_block(q):
        return aligned(q * ROWS - 16 * (q // 7), ROWS, 16)

    def head_part(a, core, source):
        return gbuf.at[a, aligned(ROWS * core, ROWS, ROWS), aligned(source * FEAT, FEAT, FEAT)]

    def head_copy(a, s, arriving):
        source = (z + NZ - s) % NZ if arriving else z
        return remote(
            heads[a].at[row_block((z + s) % NZ), :], head_part(a, c, source),
            w_send.at[a, s - 1], w_recv.at[a, s - 1], z_peers[s],
        )

    def own_rows(a):
        return pltpu.make_async_copy(
            heads[a].at[row_block(z), :], head_part(a, c, z), local_sem.at[2 + a]
        )

    def share_copy(a, s, arriving):
        part = head_part(a, 1 - c if arriving else c, (z + NZ - s) % NZ)
        return remote(part, part, s_send.at[a, s], s_recv.at[a, s], sibling)

    own_meta = pltpu.make_async_copy(meta, meta_all.at[z], local_sem.at[4])

    def home_local(q):
        return pltpu.make_async_copy(
            head_train.at[row_block(q), :], home.at[aligned(q * BOTH + c * ROWS, ROWS, ROWS), :],
            h_local.at[q],
        )

    def home_copy(q, arriving):
        core = 1 - c if arriving else c
        return remote(
            head_train.at[row_block(q), :], home.at[aligned(q * BOTH + core * ROWS, ROWS, ROWS), :],
            h_send.at[q], h_recv.at[q], sibling,
        )

    def around(peers, way):
        return peers[1 if way == 0 else len(peers) - 1]

    def back_of(step, way, arriving):
        back = step if arriving else step - 1
        return -back if way == 0 else back

    def a_copy(a, r, step, way, arriving):
        block = (y + back_of(step, way, arriving) + NY) % NY
        rows = pl.ds(TOK * r, TOK) if step < 4 else pl.ds(TOK * r + 80 * way, 80)
        part = xbuf.at[a, rows, aligned(block * FEAT, FEAT, FEAT)]
        index = (a, r, step - 1, way)
        return remote(part, part, ay_send.at[index], ay_recv.at[index], around(y_peers, way))

    def b_rows(step, last, way):
        return pl.ds(2 * TOK, 2 * TOK) if step < last else pl.ds(2 * TOK + TOK * way, TOK)

    def by_copy(a, step, way, arriving):
        block = x * NY + (y + back_of(step, way, arriving) + NY) % NY
        part = xbuf.at[a, b_rows(step, 4, way), aligned(block * PIECE, PIECE, PIECE)]
        index = (a, step - 1, way)
        return remote(part, part, by_send.at[index], by_recv.at[index], around(y_peers, way))

    def bx_copy(a, far, step, way, arriving):
        block = ((x + back_of(step, way, arriving) + NX) % NX) * NY + (y + far) % NY
        part = xbuf.at[a, b_rows(step, 2, way), aligned(block * PIECE, PIECE, PIECE)]
        index = (a, far, step - 1, way)
        return remote(part, part, bx_send.at[index], bx_recv.at[index], around(x_peers, way))

    def a_move(a, step):
        for r in (1, 0):
            def act(r=r):
                for way in (0, 1):
                    a_copy(a, r, step, way, True).wait_recv()
                    if step < 4:
                        a_copy(a, r, step + 1, way, False).start()
            when_active(r, act)

    def bx_start(a, *fars):
        for far in fars:
            for way in (0, 1):
                bx_copy(a, far % NY, 1, way, False).start()

    def bx_move(a, step, *fars):
        for far in fars:
            for way in (0, 1):
                bx_copy(a, far % NY, step, way, True).wait_recv()
                if step == 1:
                    bx_copy(a, far % NY, 2, way, False).start()

    def by_move(a, step):
        for way in (0, 1):
            by_copy(a, step, way, True).wait_recv()
            if step < 4:
                by_copy(a, step + 1, way, False).start()
        bx_start(a, *((-step, step) if step < 4 else (4,)))

    def start_rings(a):
        for r in (2, 3):
            z_arrival(a, r).wait_recv()
        for way in (0, 1):
            by_copy(a, 1, way, False).start()
        bx_start(a, 0)
        for r in (1, 0):
            def act(r=r):
                z_arrival(a, r).wait_recv()
                for way in (0, 1):
                    a_copy(a, r, 1, way, False).start()
            when_active(r, act)

    def round_of(a, number):
        if number == 0:
            start_rings(a)
        elif number == 1:
            by_move(a, 1)
        elif number == 2:
            by_move(a, 2)
            bx_move(a, 1, 0)
            a_move(a, 1)
        elif number == 3:
            by_move(a, 3)
            bx_move(a, 1, -1, 1)
        elif number == 4:
            by_move(a, 4)
            a_move(a, 2)
            bx_move(a, 1, -2, 2)
        elif number == 5:
            bx_move(a, 1, -3, 3)
            a_move(a, 3)
            bx_move(a, 1, 4)
        else:
            bx_move(a, 2, 0, -1, 1, -2, 2, -3, 3, 4)
            a_move(a, 4)

    def pass_heads(a, distances):
        for s in distances:
            head_copy(a, s, True).wait_recv()
            share_copy(a, s, False).start()

    def finish_tokens(a):
        for s in range(NZ):
            share_copy(a, s, True).wait_recv()

        @pl.when(is_source)
        def _():
            own_tokens(a).wait()

    def drain_transfers(a):
        @pl.when(is_source)
        def _():
            for s in range(1, NZ):
                z_copy(a, s).wait_send()
        for s in range(1, NZ):
            head_copy(a, s, False).wait_send()
            if a == TRAIN:
                meta_copy(s, False).wait_send()
        for s in range(NZ):
            share_copy(a, s, False).wait_send()
        for way in (0, 1):
            for step in range(1, 5):
                by_copy(a, step, way, False).wait_send()
                a_copy(a, 1, step, way, False).wait_send()
            for far in range(NY):
                for step in (1, 2):
                    bx_copy(a, far, step, way, False).wait_send()

        @pl.when(jnp.logical_not(is_source))
        def _():
            for way in (0, 1):
                for step in range(1, 5):
                    a_copy(a, 0, step, way, False).wait_send()

    def drain_home():
        for q in range(NZ):
            home_copy(q, False).wait_send()

    for a in (TRAIN, REF):
        @pl.when(is_source)
        def _():
            for s in (5, 2, 6, 1, 3, 7, 4):
                z_copy(a, s).start()
            own_tokens(a).start()
        if a == TRAIN:
            own_meta.start()
            for s in range(1, NZ):
                meta_copy(s, False).start()
        own_rows(a).start()
        for s in FAR_FIRST:
            head_copy(a, s, False).start()
    for q in range(NZ):
        home_local(q).start()
        home_copy(q, False).start()
    zero_stats = jnp.zeros((16, LANES), f32)
    for a in (REF, TRAIN):
        stats[a, 0] = zero_stats

    for number in range(4):
        round_of(TRAIN, number)
    own_rows(TRAIN).wait()
    share_copy(TRAIN, 0, False).start()
    round_of(TRAIN, 4)
    round_of(REF, 0)
    pass_heads(TRAIN, (1, 7, 2, 6))
    round_of(TRAIN, 5)
    round_of(REF, 1)
    pass_heads(TRAIN, (3, 5, 4))
    round_of(TRAIN, 6)
    own_meta.wait()
    for s in range(1, NZ):
        meta_copy(s, True).wait_recv()
    finish_tokens(TRAIN)

    row = lax.broadcasted_iota(jnp.int32, (BOTH, TOK), 0)
    within = row % ROWS
    chip = v // 2
    row_id = (2 * chip + row // ROWS) * 1008 + z * ROWS - 16 * (z // 7) + within
    valid = jnp.logical_or(within >= 16, z < 7)

    def hits(slot):
        target = lax.shift_right_logical(meta_all[4 * c + slot], 1)
        return jnp.logical_and(row_id == target, valid)

    def local_stats(a, slots):
        for r in slots:
            slot = (z + r) % 4
            table = lax.dot_general(
                gbuf[a], xbuf[a, TOK * r:TOK * (r + 1), :], LAST, preferred_element_type=f32
            )
            if a == TRAIN:
                logits[r] = table
            top = jnp.max(jnp.where(valid, table, -jnp.inf), axis=0, keepdims=True)
            parts = jnp.where(valid, jnp.exp(table - top), 0.0)
            picked = jnp.where(hits(slot), table, 0.0)
            stats[a, 0, pl.ds(slot, 1), :TOK] = top
            stats[a, 0, pl.ds(4 + slot, 1), :TOK] = jnp.sum(parts, axis=0, keepdims=True)
            stats[a, 0, pl.ds(8 + slot, 1), :TOK] = jnp.sum(picked, axis=0, keepdims=True)

    levels = (
        (z_peers, zstat, tz_send, tz_recv),
        (x_peers, xstat, tx_send, tx_recv),
        (y_peers, ystat, ty_send, ty_recv),
    )

    def stat_copies(a, level):
        peers, buf, send, recv = levels[level]
        return [
            remote(stats.at[a, level], buf.at[a, s], send.at[a, s], recv.at[a, s], peers[s + 1])
            for s in range(len(peers) - 1)
        ]

    def stat_send(a, level):
        for copy in stat_copies(a, level):
            copy.start()

    def stat_merge(a, level):
        copies = stat_copies(a, level)
        for copy in copies:
            copy.wait_recv()
        blocks = [stats[a, level]] + [levels[level][1][a, s] for s in range(len(copies))]
        top = functools.reduce(jnp.maximum, [b[0:4] for b in blocks])
        total = sum(b[4:8] * jnp.exp(b[0:4] - top) for b in blocks)
        picked = sum(b[8:12] for b in blocks)
        merged = jnp.concatenate([top, total, picked, jnp.zeros_like(top)], axis=0)
        if level < 2:
            stats[a, level + 1] = merged
        else:
            both[a, c] = merged

    def stat_share(a, arriving):
        part = both.at[a, 1 - c if arriving else c]
        return remote(part, part, tc_send.at[a], tc_recv.at[a], sibling)

    def drain_stats(a):
        for level in range(3):
            for copy in stat_copies(a, level):
                copy.wait_send()
        stat_share(a, False).wait_send()

    local_stats(TRAIN, range(4))
    stat_send(TRAIN, 0)
    round_of(REF, 2)
    stat_merge(TRAIN, 0)
    stat_send(TRAIN, 1)
    round_of(REF, 3)
    stat_merge(TRAIN, 1)
    stat_send(TRAIN, 2)
    own_rows(REF).wait()
    share_copy(REF, 0, False).start()
    stat_merge(TRAIN, 2)
    stat_share(TRAIN, False).start()

    upper = (
        lax.broadcasted_iota(jnp.int32, (TOK, TOK), 0)
        <= lax.broadcasted_iota(jnp.int32, (TOK, TOK), 1)
    ).astype(jnp.bfloat16)
    place = lax.broadcasted_iota(jnp.int32, (SLOT, TOK), 0)

    def choose(weight, place):
        count = jnp.dot(
            jnp.broadcast_to(weight, (8, TOK)).astype(jnp.bfloat16), upper,
            preferred_element_type=f32,
        )[0:1].astype(jnp.int32)
        return jnp.logical_and(place == count - 1, weight != 0)

    def slopes(b):
        for slot in (2 * b, 2 * b + 1):
            pick = choose(meta_all[4 * c + slot] & 1, place).astype(jnp.bfloat16)
            top = both[TRAIN, c, slot:slot + 1, :TOK]
            total = both[TRAIN, c, 4 + slot:5 + slot, :TOK]
            share = jnp.exp(logits[(slot + 4 - z % 4) % 4] - top) / total
            slope = jnp.where(valid, loss_scale * (share - hits(slot).astype(f32)), 0.0)
            rows = lax.dot_general(
                pick, slope.astype(jnp.bfloat16), LAST, preferred_element_type=f32
            )
            start = SLOT * (slot - 2 * b)
            gathered[z, b, start:start + SLOT, :] = rows.astype(jnp.bfloat16)

    def e_copy(b, step, way, arriving):
        rows = pl.ds(0, PAIR) if step < 4 else pl.ds(SLOT * way, SLOT)
        part = gathered.at[(z + back_of(step, way, arriving) + NZ) % NZ, b, rows, :]
        index = (b, step - 1, way)
        return remote(part, part, ez_send.at[index], ez_recv.at[index], around(z_peers, way))

    def e_move(b, step):
        for way in (0, 1):
            if step:
                e_copy(b, step, way, True).wait_recv()
            if step < 4:
                e_copy(b, step + 1, way, False).start()

    def x_copy(b, s):
        return remote(
            grad.at[b, (x + s) % NX], xgrad.at[b, s - 1], gx_send.at[b, s - 1],
            gx_recv.at[b, s - 1], x_peers[s],
        )

    def turned_part(b, q):
        return turned.at[b, q // 4, aligned((q % 4) * 32, 32, 32), :]

    def y_copy(b, s):
        return remote(
            turned_part(b, (y + s) % NY), ygrad.at[b, s - 1], gy_send.at[b, s - 1],
            gy_recv.at[b, s - 1], y_peers[s],
        )

    def final_copy(b):
        return remote(
            summed.at[b], piece.at[aligned((y % 2) * 32, 32, 32), :], f_send.at[b],
            f_recv.at[y % 2], dests[b],
        )

    def final_stay(b):
        return pltpu.make_async_copy(
            summed.at[b], piece.at[aligned((y % 2) * 32, 32, 32), :], local_sem.at[5 + b]
        )

    def multiply(b):
        columns = jnp.concatenate([gathered[q, b] for q in range(NZ)], axis=1)
        for q in range(NX):
            grad[b, q] = jnp.dot(
                columns, home[:, 128 * q:128 * (q + 1)], preferred_element_type=f32
            )
        for s in (2, 1, 3):
            x_copy(b, s).start()

    def turn(b):
        for s in range(1, NX):
            x_copy(b, s).wait_recv()
        total = grad[b, x] + xgrad[b, 0] + xgrad[b, 1] + xgrad[b, 2]
        for i in (0, 1):
            block = jnp.concatenate(
                [total[SLOT * i:SLOT * (i + 1)], jnp.zeros((128 - SLOT, 128), f32)], axis=0
            )
            turned[b, i] = block.T
        for s in FAR_FIRST:
            y_copy(b, s).start()

    def hand_over(b):
        for s in range(1, NY):
            y_copy(b, s).wait_recv()
        summed[b] = turned_part(b, y)[...] + sum(ygrad[b, s] for s in range(NY - 1))

        @pl.when(jnp.logical_not(is_here(dests[b])))
        def _():
            final_copy(b).start()

        @pl.when(is_here(dests[b]))
        def _():
            final_stay(b).start()
            final_stay(b).wait()

    def drain_grads():
        for b in (0, 1):
            for way in (0, 1):
                for step in range(1, 5):
                    e_copy(b, step, way, False).wait_send()
            for s in range(1, NX):
                x_copy(b, s).wait_send()
            for s in range(1, NY):
                y_copy(b, s).wait_send()

            @pl.when(jnp.logical_not(is_here(dests[b])))
            def _():
                final_copy(b).wait_send()

    slopes(0)
    e_move(0, 0)
    slopes(1)
    e_move(1, 0)
    round_of(REF, 4)
    e_move(0, 1)
    pass_heads(REF, (1, 7, 2))
    e_move(1, 1)
    e_move(0, 2)
    round_of(REF, 5)
    pass_heads(REF, (6, 3))
    e_move(1, 2)
    e_move(0, 3)
    pass_heads(REF, (5, 4))
    e_move(1, 3)
    for q in range(NZ):
        home_local(q).wait()
        home_copy(q, True).wait_recv()
    e_move(0, 4)
    multiply(0)
    round_of(REF, 6)
    finish_tokens(REF)
    local_stats(REF, (0, 1))
    e_move(1, 4)
    multiply(1)
    local_stats(REF, (2, 3))
    stat_send(REF, 0)
    turn(0)
    turn(1)
    stat_merge(REF, 0)
    stat_send(REF, 1)
    hand_over(0)
    hand_over(1)
    stat_merge(REF, 1)
    stat_send(REF, 2)
    for h in (0, 1):
        @pl.when(jnp.logical_not(is_here(origins[h])))
        def _():
            part = piece.at[pl.ds(32 * h, 32), :]
            remote(part, part, f_send.at[0], f_recv.at[h], sibling).wait_recv()
    own_place = choose(
        meta_all[z] & 1, lax.broadcasted_iota(jnp.int32, (128, TOK), 0)
    ).astype(f32)
    grad_out[...] = jnp.dot(
        piece[...], own_place, precision=lax.Precision.HIGHEST, preferred_element_type=f32
    )
    stat_merge(REF, 2)
    stat_share(REF, False).start()
    for a in (TRAIN, REF):
        stat_share(a, True).wait_recv()

    def cross(block, first, count):
        top = block[pl.ds(first, count), :TOK]
        total = block[pl.ds(4 + first, count), :TOK]
        return jnp.log(total) + top - block[pl.ds(8 + first, count), :TOK]

    excess_out[...] = cross(both.at[TRAIN, z // 4], z % 4, 1) - cross(
        both.at[REF, z // 4], z % 4, 1
    )
    loss = jnp.zeros((1, 1), f32)
    for h in (0, 1):
        weight = jnp.concatenate([meta_all[4 * h + i] & 1 for i in range(4)], axis=0)
        loss = loss + jnp.sum(
            weight.astype(f32) * cross(both.at[TRAIN, h], 0, 4), axis=(0, 1), keepdims=True
        )
    loss_out[...] = jnp.broadcast_to(loss / (NZ * SEL), loss_out.shape)

    for a in (REF, TRAIN):
        drain_transfers(a)
        drain_stats(a)
    drain_home()
    drain_grads()


def fused(hidden_ref, hidden_train, head_ref, head_train, meta):
    anywhere = pl.BlockSpec(memory_space=pl.ANY)
    vmem = pl.BlockSpec(memory_space=pltpu.VMEM)
    dma = pltpu.SemaphoreType.DMA
    sds = jax.ShapeDtypeStruct
    f32, bf16 = jnp.float32, jnp.bfloat16
    buf = pltpu.VMEM
    pairs = [
        (2, NZ - 1), (2, 4), (NZ - 1,), (NZ - 1,), (2, NZ - 1), (2, NZ - 1), (2, NZ), (2, NZ),
        (NZ,), (NZ,), (NZ,), (2, 2, 4, 2), (2, 2, 4, 2), (2, 4, 2), (2, 4, 2),
        (2, NY, 2, 2), (2, NY, 2, 2),
        (2, NZ - 1), (2, NZ - 1), (2, NX - 1), (2, NX - 1), (2, NY - 1), (2, NY - 1), (2,), (2,),
        (2, 4, 2), (2, 4, 2), (2, NX - 1), (2, NX - 1), (2, NY - 1), (2, NY - 1), (2,), (2,),
    ]
    return pl.pallas_call(
        kernel,
        out_shape=[sds((64, TOK), f32), sds((1, TOK), f32), sds((1, 128), f32)],
        in_specs=[anywhere] * 5,
        out_specs=[vmem] * 3,
        scratch_shapes=[
            buf((NZ, 1, TOK), jnp.int32), buf((2, 2, 16, LANES), f32),
            buf((2, 4 * TOK, WIDTH), bf16), buf((2, BOTH, WIDTH), bf16),
            buf((NZ * BOTH, FEAT), bf16), buf((4, BOTH, TOK), f32),
            buf((2, 3, 16, LANES), f32), buf((2, NZ - 1, 16, LANES), f32),
            buf((2, NX - 1, 16, LANES), f32), buf((2, NY - 1, 16, LANES), f32),
            buf((NZ, 2, PAIR, BOTH), bf16), buf((2, NX, PAIR, 128), f32),
            buf((2, NX - 1, PAIR, 128), f32), buf((2, 2, 128, 128), f32),
            buf((2, NY - 1, 32, 128), f32), buf((2, 32, 128), f32), buf((64, 128), f32),
            dma((7,)), *[dma(shape) for shape in pairs],
        ],
        compiler_params=pltpu.CompilerParams(
            collective_id=0, has_side_effects=True, vmem_limit_bytes=60 * 1024 * 1024
        ),
        name="fused",
    )(hidden_ref, hidden_train, head_ref, head_train, meta)


def body(hidden_ref, hidden_train, head_ref, head_train, targets, mask):
    meta = (2 * targets + mask).reshape(1, TOK)
    hidden_grad, excess, loss = fused(hidden_ref, hidden_train, head_ref, head_train, meta)
    return (excess.reshape(TOK), loss[0, 0], hidden_grad)


def solution(mesh):
    in_specs = (P("dp", None), P("dp", None), P("vocab", "dp"), P("vocab", "dp"), P("dp"), P("dp"))
    out_specs = (P("dp"), P(), P("vocab", "dp"))
    return jax.shard_map(body, mesh=mesh, in_specs=in_specs, out_specs=out_specs, check_vma=False)
```

time: 626 us -> 156 us (0.25)
  waiting for transfers between devices: 312 us -> 0 us
  blocking collectives: 265 us -> 0 us
  Pallas kernels: 0 us -> 150 us
  matrix products: 17.5 us -> 0 us
  between operations: 15.6 us -> 2.33 us
    all_gather x2 -> x0, waiting for transfers between devices: 190 us -> none  [the longest x1 99.4 us: body(): lax.all_gather(head_ref, 'dp', axis=1, tiled=True)]
    pallas_call x0 -> x1, Pallas kernels: none -> 150 us  [fused(): pl.pallas_call(kernel, out_shape=[sds((64, TOK), f32), sds((1, TOK), f32)...]
    psum x2 -> x0, blocking collectives: 141 us -> none  [the longest x1 128 us: body(): lax.psum((jnp.sum(jnp.exp(ref_logits - ref_max[:, None]), axis=1), jnp.su...]
    pmax x1 -> x0, blocking collectives: 124 us -> none  [body(): ref_max, train_max = lax.pmax((local_ref_max, local_train_max), 'vocab')]
    unnamed x4 -> x0, waiting for transfers between devices: 123 us -> none
    dot_general x3 -> x0, matrix products: 17.5 us -> none  [the longest x1 6.61 us: body(): lax.dot_general(hidden_train, trained_slab, contract_last, preferred_elem...]
  transfers between devices with their start and end apart: 3 -> 0, of which waited for: 3 -> 0; matrix products, arithmetic and copies ran while one was open for 2% -> 0% of each run, Pallas kernels for 0% -> 0%
where the time goes in v3:
time: 156 us
  Pallas kernels  150 us (96%)
  local copies, waits for them, and re-layouts  2.67 us (2%)
  between operations  2.33 us (1%)
    pallas_call x1, Pallas kernels, fused(): pl.pallas_call(kernel, out_shape=[sds((64, TOK), f32), sds((1, TOK), f32)...  150 us

profile of v3, /device:TPU:1, one launch (start us, length us, event | category | flops | bytes accessed | tf_op | source)
XLA Modules:
  0.0 156.3 jit_solution(11160669710069036943)
XLA Ops:
  0.6 1.3 multiply_add_fusion
  1.9 150.0 %fused.1 = (f32[64,160]{1,0:T(8,128)}, f32[1,160]{1,0:T(1,128)}, f32[1,128]{1,0:T(1,128)}) custom-call(bf16[160,4096]{1,0:T(8,128)(2,1)} %hid_ref.1, bf16[160,4096]{1,0:T(8,128)(2,1)} %hid_train.1, bf16[1008,512]{1,0:T(8,128)(2,1)} %head_ref.1, bf16[1008,512]{1,0:T(8,128)(2,1)} %head_train.1, s32[1,160]{1,0:T(1,128)} %bitcast.4), custom_call_target="tpu_custom_call" | custom-call | tf_op jit(solution)/shard_map/fused/pallas_call | solution.py:612
  151.9 1.2 copy.12
  153.7 1.5 copy.14

commit v4 on v3

--- a/solution.py
+++ b/solution.py
@@ -21,6 +21,9 @@
 LANES = 256
 BOTH = 2 * ROWS
 FAR_FIRST = (4, 3, 5, 2, 6, 1, 7)
+NEAR_FIRST = (1, 7, 2, 6, 3, 5, 4)
+REF_FIRST = (2, 6, 1, 7)
+REF_LATER = (3, 5, 4)
 LAST = (((1,), (1,)), ((), ()))
 REF, TRAIN = 0, 1
 
@@ -47,12 +50,12 @@
 
 
 def kernel(
-    hid_ref, hid_train, head_ref, head_train, meta,
+    hid_ref, hid_train, head_ref, head_train, targets, mask,
     grad_out, excess_out, loss_out,
-    meta_all, both, xbuf, gbuf, home, logits, stats, zstat, xstat, ystat,
-    gathered, grad, xgrad, turned, ygrad, summed, piece,
+    meta, meta_all, stats_t, zstat_t, xstat_t, ystat_t, both_t,
+    stats_r, zstat_r, xstat_r, ystat_r, both_r, xbuf, gbuf, home, logits, gathered, grad, xgrad, turned, ygrad, summed, piece,
     local_sem, z_send, z_recv, m_send, m_recv, w_send, w_recv, s_send, s_recv,
-    h_local, h_send, h_recv, ay_send, ay_recv, by_send, by_recv, bx_send, bx_recv,
+    h_local, h_send, h_recv, ax_send, ax_recv, ay_send, ay_recv, by_send, by_recv, bx_send, bx_recv,
     tz_send, tz_recv, tx_send, tx_recv, ty_send, ty_recv, tc_send, tc_recv,
     ez_send, ez_recv, gx_send, gx_recv, gy_send, gy_recv, f_send, f_recv,
 ):
@@ -85,6 +88,8 @@
 
     pl.semaphore_wait(barrier, expected)
 
+    meta[...] = 2 * targets[...] + mask[...]
+
     is_source = z // 4 == c
     hid = (hid_ref, hid_train)
     heads = (head_ref, head_train)
@@ -97,7 +102,7 @@
 
     def z_columns(r):
         if r < 2:
-            return aligned(y * FEAT, FEAT, FEAT)
+            return aligned((y * NX + x) * PIECE, PIECE, PIECE)
         return aligned((x * NY + y) * PIECE, PIECE, PIECE)
 
     def z_copy(a, s):
@@ -163,6 +168,13 @@
         back = step if arriving else step - 1
         return -back if way == 0 else back
 
+    def ax_copy(a, r, step, way, arriving):
+        block = y * NX + (x + back_of(step, way, arriving) + NX) % NX
+        rows = pl.ds(TOK * r, TOK) if step < 2 else pl.ds(TOK * r + 80 * way, 80)
+        part = xbuf.at[a, rows, aligned(block * PIECE, PIECE, PIECE)]
+        index = (a, r, step - 1, way)
+        return remote(part, part, ax_send.at[index], ax_recv.at[index], around(x_peers, way))
+
     def a_copy(a, r, step, way, arriving):
         block = (y + back_of(step, way, arriving) + NY) % NY
         rows = pl.ds(TOK * r, TOK) if step < 4 else pl.ds(TOK * r + 80 * way, 80)
@@ -184,6 +196,19 @@
         part = xbuf.at[a, b_rows(step, 2, way), aligned(block * PIECE, PIECE, PIECE)]
         index = (a, far, step - 1, way)
         return remote(part, part, bx_send.at[index], bx_recv.at[index], around(x_peers, way))
+
+    def ax_move(a, step):
+        for r in (1, 0):
+            def act(r=r):
+                for way in (0, 1):
+                    if step:
+                        ax_copy(a, r, step, way, True).wait_recv()
+                    if step < 2:
+                        ax_copy(a, r, step + 1, way, False).start()
+                if step == 2:
+                    for way in (0, 1):
+                        a_copy(a, r, 1, way, False).start()
+            when_active(r, act)
 
     def a_move(a, step):
         for r in (1, 0):
@@ -213,39 +238,34 @@
                 by_copy(a, step + 1, way, False).start()
         bx_start(a, *((-step, step) if step < 4 else (4,)))
 
-    def start_rings(a):
-        for r in (2, 3):
-            z_arrival(a, r).wait_recv()
-        for way in (0, 1):
-            by_copy(a, 1, way, False).start()
-        bx_start(a, 0)
-        for r in (1, 0):
-            def act(r=r):
-                z_arrival(a, r).wait_recv()
-                for way in (0, 1):
-                    a_copy(a, r, 1, way, False).start()
-            when_active(r, act)
-
     def round_of(a, number):
         if number == 0:
-            start_rings(a)
+            for r in (2, 3):
+                z_arrival(a, r).wait_recv()
+            for way in (0, 1):
+                by_copy(a, 1, way, False).start()
+            bx_start(a, 0)
+            for r in (1, 0):
+                when_active(r, lambda r=r: z_arrival(a, r).wait_recv())
+            ax_move(a, 0)
         elif number == 1:
             by_move(a, 1)
+            ax_move(a, 1)
         elif number == 2:
             by_move(a, 2)
+            ax_move(a, 2)
             bx_move(a, 1, 0)
-            a_move(a, 1)
         elif number == 3:
             by_move(a, 3)
             bx_move(a, 1, -1, 1)
         elif number == 4:
             by_move(a, 4)
-            a_move(a, 2)
+            a_move(a, 1)
             bx_move(a, 1, -2, 2)
         elif number == 5:
-            bx_move(a, 1, -3, 3)
+            a_move(a, 2)
+            bx_move(a, 1, -3, 3, 4)
             a_move(a, 3)
-            bx_move(a, 1, 4)
         else:
             bx_move(a, 2, 0, -1, 1, -2, 2, -3, 3, 4)
             a_move(a, 4)
@@ -277,56 +297,64 @@
         for way in (0, 1):
             for step in range(1, 5):
                 by_copy(a, step, way, False).wait_send()
-                a_copy(a, 1, step, way, False).wait_send()
             for far in range(NY):
                 for step in (1, 2):
                     bx_copy(a, far, step, way, False).wait_send()
-
-        @pl.when(jnp.logical_not(is_source))
-        def _():
-            for way in (0, 1):
-                for step in range(1, 5):
-                    a_copy(a, 0, step, way, False).wait_send()
+        for r in (0, 1):
+            def act(r=r):
+                for way in (0, 1):
+                    for step in (1, 2):
+                        ax_copy(a, r, step, way, False).wait_send()
+                    for step in range(1, 5):
+                        a_copy(a, r, step, way, False).wait_send()
+            when_active(r, act)
 
     def drain_home():
         for q in range(NZ):
             home_copy(q, False).wait_send()
 
-    for a in (TRAIN, REF):
+    def send_tokens(a):
         @pl.when(is_source)
         def _():
             for s in (5, 2, 6, 1, 3, 7, 4):
                 z_copy(a, s).start()
             own_tokens(a).start()
-        if a == TRAIN:
-            own_meta.start()
-            for s in range(1, NZ):
-                meta_copy(s, False).start()
-        own_rows(a).start()
-        for s in FAR_FIRST:
+
+    def send_heads(a, distances):
+        for s in distances:
             head_copy(a, s, False).start()
+
+    send_tokens(TRAIN)
+    own_meta.start()
+    for s in range(1, NZ):
+        meta_copy(s, False).start()
+    own_rows(TRAIN).start()
+    own_rows(REF).start()
+    stats_t[0] = jnp.zeros((8, LANES), f32)
+    stats_r[0] = jnp.zeros((16, LANES), f32)
+    round_of(TRAIN, 0)
+    send_heads(TRAIN, FAR_FIRST)
+    round_of(TRAIN, 1)
+    own_rows(TRAIN).wait()
+    share_copy(TRAIN, 0, False).start()
+    own_rows(REF).wait()
+    share_copy(REF, 0, False).start()
+    round_of(TRAIN, 2)
     for q in range(NZ):
         home_local(q).start()
         home_copy(q, False).start()
-    zero_stats = jnp.zeros((16, LANES), f32)
-    for a in (REF, TRAIN):
-        stats[a, 0] = zero_stats
-
-    for number in range(4):
+    for number in (3, 4, 5):
         round_of(TRAIN, number)
-    own_rows(TRAIN).wait()
-    share_copy(TRAIN, 0, False).start()
-    round_of(TRAIN, 4)
+    pass_heads(TRAIN, NEAR_FIRST)
+    send_tokens(REF)
+    send_heads(REF, FAR_FIRST)
     round_of(REF, 0)
-    pass_heads(TRAIN, (1, 7, 2, 6))
-    round_of(TRAIN, 5)
-    round_of(REF, 1)
-    pass_heads(TRAIN, (3, 5, 4))
     round_of(TRAIN, 6)
     own_meta.wait()
     for s in range(1, NZ):
         meta_copy(s, True).wait_recv()
     finish_tokens(TRAIN)
+    round_of(REF, 1)
 
     row = lax.broadcasted_iota(jnp.int32, (BOTH, TOK), 0)
     within = row % ROWS
@@ -349,20 +377,23 @@
             top = jnp.max(jnp.where(valid, table, -jnp.inf), axis=0, keepdims=True)
             parts = jnp.where(valid, jnp.exp(table - top), 0.0)
             picked = jnp.where(hits(slot), table, 0.0)
-            stats[a, 0, pl.ds(slot, 1), :TOK] = top
-            stats[a, 0, pl.ds(4 + slot, 1), :TOK] = jnp.sum(parts, axis=0, keepdims=True)
-            stats[a, 0, pl.ds(8 + slot, 1), :TOK] = jnp.sum(picked, axis=0, keepdims=True)
-
-    levels = (
-        (z_peers, zstat, tz_send, tz_recv),
-        (x_peers, xstat, tx_send, tx_recv),
-        (y_peers, ystat, ty_send, ty_recv),
+            mine = (stats_r, stats_t)[a]
+            mine[0, pl.ds(slot, 1), :TOK] = top
+            mine[0, pl.ds(4 + slot, 1), :TOK] = jnp.sum(parts, axis=0, keepdims=True)
+            stats_r[0, pl.ds(8 + 4 * a + slot, 1), :TOK] = jnp.sum(picked, axis=0, keepdims=True)
+
+    sums = (
+        ((stats_r, zstat_r, xstat_r, ystat_r), both_r), ((stats_t, zstat_t, xstat_t, ystat_t), both_t)
     )
+    hops = ((z_peers, tz_send, tz_recv), (x_peers, tx_send, tx_recv), (y_peers, ty_send, ty_recv))
 
     def stat_copies(a, level):
-        peers, buf, send, recv = levels[level]
+        peers, send, recv = hops[level]
+        bufs = sums[a][0]
         return [
-            remote(stats.at[a, level], buf.at[a, s], send.at[a, s], recv.at[a, s], peers[s + 1])
+            remote(
+                bufs[0].at[level], bufs[level + 1].at[s], send.at[a, s], recv.at[a, s], peers[s + 1]
+            )
             for s in range(len(peers) - 1)
         ]
 
@@ -371,21 +402,21 @@
             copy.start()
 
     def stat_merge(a, level):
+        bufs, result = sums[a]
         copies = stat_copies(a, level)
         for copy in copies:
             copy.wait_recv()
-        blocks = [stats[a, level]] + [levels[level][1][a, s] for s in range(len(copies))]
+        blocks = [bufs[0][level]] + [bufs[level + 1][s] for s in range(len(copies))]
         top = functools.reduce(jnp.maximum, [b[0:4] for b in blocks])
         total = sum(b[4:8] * jnp.exp(b[0:4] - top) for b in blocks)
-        picked = sum(b[8:12] for b in blocks)
-        merged = jnp.concatenate([top, total, picked, jnp.zeros_like(top)], axis=0)
+        merged = jnp.concatenate([top, total] + [sum(b[8:] for b in blocks)] * (1 - a), axis=0)
         if level < 2:
-            stats[a, level + 1] = merged
+            bufs[0][level + 1] = merged
         else:
-            both[a, c] = merged
+            result[c] = merged
 
     def stat_share(a, arriving):
-        part = both.at[a, 1 - c if arriving else c]
+        part = sums[a][1].at[1 - c if arriving else c]
         return remote(part, part, tc_send.at[a], tc_recv.at[a], sibling)
 
     def drain_stats(a):
@@ -402,8 +433,8 @@
     round_of(REF, 3)
     stat_merge(TRAIN, 1)
     stat_send(TRAIN, 2)
-    own_rows(REF).wait()
-    share_copy(REF, 0, False).start()
+    round_of(REF, 4)
+    pass_heads(REF, REF_FIRST)
     stat_merge(TRAIN, 2)
     stat_share(TRAIN, False).start()
 
@@ -423,8 +454,8 @@
     def slopes(b):
         for slot in (2 * b, 2 * b + 1):
             pick = choose(meta_all[4 * c + slot] & 1, place).astype(jnp.bfloat16)
-            top = both[TRAIN, c, slot:slot + 1, :TOK]
-            total = both[TRAIN, c, 4 + slot:5 + slot, :TOK]
+            top = both_t[c, slot:slot + 1, :TOK]
+            total = both_t[c, 4 + slot:5 + slot, :TOK]
             share = jnp.exp(logits[(slot + 4 - z % 4) % 4] - top) / total
             slope = jnp.where(valid, loss_scale * (share - hits(slot).astype(f32)), 0.0)
             rows = lax.dot_general(
@@ -525,28 +556,24 @@
     e_move(0, 0)
     slopes(1)
     e_move(1, 0)
-    round_of(REF, 4)
     e_move(0, 1)
-    pass_heads(REF, (1, 7, 2))
     e_move(1, 1)
+    round_of(REF, 5)
     e_move(0, 2)
-    round_of(REF, 5)
-    pass_heads(REF, (6, 3))
     e_move(1, 2)
+    pass_heads(REF, REF_LATER)
     e_move(0, 3)
-    pass_heads(REF, (5, 4))
     e_move(1, 3)
     for q in range(NZ):
         home_local(q).wait()
         home_copy(q, True).wait_recv()
     e_move(0, 4)
     multiply(0)
+    e_move(1, 4)
+    multiply(1)
     round_of(REF, 6)
     finish_tokens(REF)
-    local_stats(REF, (0, 1))
-    e_move(1, 4)
-    multiply(1)
-    local_stats(REF, (2, 3))
+    local_stats(REF, range(4))
     stat_send(REF, 0)
     turn(0)
     turn(1)
@@ -572,19 +599,18 @@
     for a in (TRAIN, REF):
         stat_share(a, True).wait_recv()
 
-    def cross(block, first, count):
+    def cross(a, h, first, count):
+        block = sums[a][1].at[h]
         top = block[pl.ds(first, count), :TOK]
         total = block[pl.ds(4 + first, count), :TOK]
-        return jnp.log(total) + top - block[pl.ds(8 + first, count), :TOK]
-
-    excess_out[...] = cross(both.at[TRAIN, z // 4], z % 4, 1) - cross(
-        both.at[REF, z // 4], z % 4, 1
-    )
+        return jnp.log(total) + top - both_r[h, pl.ds(8 + 4 * a + first, count), :TOK]
+
+    excess_out[...] = cross(TRAIN, z // 4, z % 4, 1) - cross(REF, z // 4, z % 4, 1)
     loss = jnp.zeros((1, 1), f32)
     for h in (0, 1):
         weight = jnp.concatenate([meta_all[4 * h + i] & 1 for i in range(4)], axis=0)
         loss = loss + jnp.sum(
-            weight.astype(f32) * cross(both.at[TRAIN, h], 0, 4), axis=(0, 1), keepdims=True
+            weight.astype(f32) * cross(TRAIN, h, 0, 4), axis=(0, 1), keepdims=True
         )
     loss_out[...] = jnp.broadcast_to(loss / (NZ * SEL), loss_out.shape)
 
@@ -595,7 +621,7 @@
     drain_grads()
 
 
-def fused(hidden_ref, hidden_train, head_ref, head_train, meta):
+def fused(hidden_ref, hidden_train, head_ref, head_train, targets, mask):
     anywhere = pl.BlockSpec(memory_space=pl.ANY)
     vmem = pl.BlockSpec(memory_space=pltpu.VMEM)
     dma = pltpu.SemaphoreType.DMA
@@ -604,7 +630,7 @@
     buf = pltpu.VMEM
     pairs = [
         (2, NZ - 1), (2, 4), (NZ - 1,), (NZ - 1,), (2, NZ - 1), (2, NZ - 1), (2, NZ), (2, NZ),
-        (NZ,), (NZ,), (NZ,), (2, 2, 4, 2), (2, 2, 4, 2), (2, 4, 2), (2, 4, 2),
+        (NZ,), (NZ,), (NZ,), (2, 2, 2, 2), (2, 2, 2, 2), (2, 2, 4, 2), (2, 2, 4, 2), (2, 4, 2), (2, 4, 2),
         (2, NY, 2, 2), (2, NY, 2, 2),
         (2, NZ - 1), (2, NZ - 1), (2, NX - 1), (2, NX - 1), (2, NY - 1), (2, NY - 1), (2,), (2,),
         (2, 4, 2), (2, 4, 2), (2, NX - 1), (2, NX - 1), (2, NY - 1), (2, NY - 1), (2,), (2,),
@@ -612,14 +638,16 @@
     return pl.pallas_call(
         kernel,
         out_shape=[sds((64, TOK), f32), sds((1, TOK), f32), sds((1, 128), f32)],
-        in_specs=[anywhere] * 5,
+        in_specs=[anywhere] * 4 + [vmem] * 2,
         out_specs=[vmem] * 3,
         scratch_shapes=[
-            buf((NZ, 1, TOK), jnp.int32), buf((2, 2, 16, LANES), f32),
+            buf((1, TOK), jnp.int32), buf((NZ, 1, TOK), jnp.int32),
+            *[
+                buf((count, rows, LANES), f32)
+                for rows in (8, 16) for count in (3, NZ - 1, NX - 1, NY - 1, 2)
+            ],
             buf((2, 4 * TOK, WIDTH), bf16), buf((2, BOTH, WIDTH), bf16),
             buf((NZ * BOTH, FEAT), bf16), buf((4, BOTH, TOK), f32),
-            buf((2, 3, 16, LANES), f32), buf((2, NZ - 1, 16, LANES), f32),
-            buf((2, NX - 1, 16, LANES), f32), buf((2, NY - 1, 16, LANES), f32),
             buf((NZ, 2, PAIR, BOTH), bf16), buf((2, NX, PAIR, 128), f32),
             buf((2, NX - 1, PAIR, 128), f32), buf((2, 2, 128, 128), f32),
             buf((2, NY - 1, 32, 128), f32), buf((2, 32, 128), f32), buf((64, 128), f32),
@@ -629,12 +657,14 @@
             collective_id=0, has_side_effects=True, vmem_limit_bytes=60 * 1024 * 1024
         ),
         name="fused",
-    )(hidden_ref, hidden_train, head_ref, head_train, meta)
+    )(hidden_ref, hidden_train, head_ref, head_train, targets, mask)
 
 
 def body(hidden_ref, hidden_train, head_ref, head_train, targets, mask):
-    meta = (2 * targets + mask).reshape(1, TOK)
-    hidden_grad, excess, loss = fused(hidden_ref, hidden_train, head_ref, head_train, meta)
+    hidden_grad, excess, loss = fused(
+        hidden_ref, hidden_train, head_ref, head_train,
+        targets.reshape(1, TOK), mask.reshape(1, TOK),
+    )
     return (excess.reshape(TOK), loss[0, 0], hidden_grad)
 
 

time: 156 us -> 147 us (0.942)
  Pallas kernels: 150 us -> 142 us
    pallas_call x1, Pallas kernels: 150 us -> 142 us  [fused(): pl.pallas_call(kernel, out_shape=[sds((64, TOK), f32), sds((1, TOK), f32)...]
where the time goes in v4:
time: 147 us
  Pallas kernels  142 us (97%)
  local copies, waits for them, and re-layouts  2.67 us (2%)
  between operations  2.33 us (2%)
    pallas_call x1, Pallas kernels, fused(): pl.pallas_call(kernel, out_shape=[sds((64, TOK), f32), sds((1, TOK), f32)...  142 us

profile of v4, /device:TPU:1, one launch (start us, length us, event | category | flops | bytes accessed | tf_op | source)
XLA Modules:
  0.0 146.5 jit_solution(8912826430302861234)
XLA Ops:
  0.6 141.5 %fused.1 = (f32[64,160]{1,0:T(8,128)}, f32[1,160]{1,0:T(1,128)}, f32[1,128]{1,0:T(1,128)}) custom-call(bf16[160,4096]{1,0:T(8,128)(2,1)} %hid_ref.1, bf16[160,4096]{1,0:T(8,128)(2,1)} %hid_train.1, bf16[1008,512]{1,0:T(8,128)(2,1)} %head_ref.1, bf16[1008,512]{1,0:T(8,128)(2,1)} %head_train.1, s32[1,160]{1,0:T(1,128)} %bitcast.6, s32[1,160]{1,0:T(1,128)} %bitcast.7), custom_call_target="tpu_custom_call" | custom-call | tf_op jit(solution)/shard_map/fused/pallas_call | solution.py:638
  142.2 1.2 copy.12
  143.9 1.5 %copy.14 = f32[64,160]{1,0:T(8,128)} copy(f32[64,160]{1,0:T(8,128)} %get-tuple-element.14) | data formatting | bytes 81920

commit v5 on v4

--- a/solution.py
+++ b/solution.py
@@ -22,8 +22,6 @@
 BOTH = 2 * ROWS
 FAR_FIRST = (4, 3, 5, 2, 6, 1, 7)
 NEAR_FIRST = (1, 7, 2, 6, 3, 5, 4)
-REF_FIRST = (2, 6, 1, 7)
-REF_LATER = (3, 5, 4)
 LAST = (((1,), (1,)), ((), ()))
 REF, TRAIN = 0, 1
 
@@ -343,18 +341,19 @@
     for q in range(NZ):
         home_local(q).start()
         home_copy(q, False).start()
-    for number in (3, 4, 5):
-        round_of(TRAIN, number)
+    round_of(TRAIN, 3)
+    send_tokens(REF)
+    send_heads(REF, (4, 1, 7))
+    round_of(TRAIN, 4)
+    round_of(TRAIN, 5)
     pass_heads(TRAIN, NEAR_FIRST)
-    send_tokens(REF)
-    send_heads(REF, FAR_FIRST)
     round_of(REF, 0)
     round_of(TRAIN, 6)
+    round_of(REF, 1)
     own_meta.wait()
     for s in range(1, NZ):
         meta_copy(s, True).wait_recv()
     finish_tokens(TRAIN)
-    round_of(REF, 1)
 
     row = lax.broadcasted_iota(jnp.int32, (BOTH, TOK), 0)
     within = row % ROWS
@@ -430,11 +429,10 @@
     round_of(REF, 2)
     stat_merge(TRAIN, 0)
     stat_send(TRAIN, 1)
+    send_heads(REF, (3, 5))
     round_of(REF, 3)
     stat_merge(TRAIN, 1)
     stat_send(TRAIN, 2)
-    round_of(REF, 4)
-    pass_heads(REF, REF_FIRST)
     stat_merge(TRAIN, 2)
     stat_share(TRAIN, False).start()
 
@@ -556,14 +554,17 @@
     e_move(0, 0)
     slopes(1)
     e_move(1, 0)
+    round_of(REF, 4)
     e_move(0, 1)
     e_move(1, 1)
-    round_of(REF, 5)
+    pass_heads(REF, (1, 7, 4))
     e_move(0, 2)
     e_move(1, 2)
-    pass_heads(REF, REF_LATER)
+    round_of(REF, 5)
+    pass_heads(REF, (3, 5))
     e_move(0, 3)
     e_move(1, 3)
+    send_heads(REF, (2, 6))
     for q in range(NZ):
         home_local(q).wait()
         home_copy(q, True).wait_recv()
@@ -571,6 +572,7 @@
     multiply(0)
     e_move(1, 4)
     multiply(1)
+    pass_heads(REF, (2, 6))
     round_of(REF, 6)
     finish_tokens(REF)
     local_stats(REF, range(4))

time: 147 us -> 136 us (0.925)
  Pallas kernels: 142 us -> 131 us
    pallas_call x1, Pallas kernels: 142 us -> 131 us  [fused(): pl.pallas_call(kernel, out_shape=[sds((64, TOK), f32), sds((1, TOK), f32)...]
where the time goes in v5:
time: 136 us
  Pallas kernels  131 us (96%)
  local copies, waits for them, and re-layouts  2.67 us (2%)
  between operations  2.33 us (2%)
    pallas_call x1, Pallas kernels, fused(): pl.pallas_call(kernel, out_shape=[sds((64, TOK), f32), sds((1, TOK), f32)...  131 us

profile of v5, /device:TPU:1, one launch (start us, length us, event | category | flops | bytes accessed | tf_op | source)
XLA Modules:
  0.0 136.2 jit_solution(6747506382065196667)
XLA Ops:
  0.6 131.2 %fused.1 = (f32[64,160]{1,0:T(8,128)}, f32[1,160]{1,0:T(1,128)}, f32[1,128]{1,0:T(1,128)}) custom-call(bf16[160,4096]{1,0:T(8,128)(2,1)} %hid_ref.1, bf16[160,4096]{1,0:T(8,128)(2,1)} %hid_train.1, bf16[1008,512]{1,0:T(8,128)(2,1)} %head_ref.1, bf16[1008,512]{1,0:T(8,128)(2,1)} %head_train.1, s32[1,160]{1,0:T(1,128)} %bitcast.6, s32[1,160]{1,0:T(1,128)} %bitcast.7), custom_call_target="tpu_custom_call" | custom-call | tf_op jit(solution)/shard_map/fused/pallas_call | solution.py:640
  131.8 1.2 copy.12
  133.6 1.5 %copy.14 = f32[64,160]{1,0:T(8,128)} copy(f32[64,160]{1,0:T(8,128)} %get-tuple-element.14) | data formatting | bytes 81920

commit v6 on v5

--- a/solution.py
+++ b/solution.py
@@ -568,6 +568,9 @@
     for q in range(NZ):
         home_local(q).wait()
         home_copy(q, True).wait_recv()
+    drain_transfers(TRAIN)
+    drain_stats(TRAIN)
+    drain_home()
     e_move(0, 4)
     multiply(0)
     e_move(1, 4)
@@ -585,6 +588,7 @@
     hand_over(1)
     stat_merge(REF, 1)
     stat_send(REF, 2)
+    drain_transfers(REF)
     for h in (0, 1):
         @pl.when(jnp.logical_not(is_here(origins[h])))
         def _():
@@ -616,10 +620,7 @@
         )
     loss_out[...] = jnp.broadcast_to(loss / (NZ * SEL), loss_out.shape)
 
-    for a in (REF, TRAIN):
-        drain_transfers(a)
-        drain_stats(a)
-    drain_home()
+    drain_stats(REF)
     drain_grads()
 
 

time: 136 us -> 136 us (level)
  no operation moved by 1% of the time
where the time goes in v6:
time: 136 us
  Pallas kernels  131 us (96%)
  local copies, waits for them, and re-layouts  2.67 us (2%)
  between operations  2.33 us (2%)
    pallas_call x1, Pallas kernels, fused(): pl.pallas_call(kernel, out_shape=[sds((64, TOK), f32), sds((1, TOK), f32)...  131 us

profile of v6, /device:TPU:1, one launch (start us, length us, event | category | flops | bytes accessed | tf_op | source)
XLA Modules:
  0.0 135.9 jit_solution(6819179148199618662)
XLA Ops:
  0.6 130.9 %fused.1 = (f32[64,160]{1,0:T(8,128)}, f32[1,160]{1,0:T(1,128)}, f32[1,128]{1,0:T(1,128)}) custom-call(bf16[160,4096]{1,0:T(8,128)(2,1)} %hid_ref.1, bf16[160,4096]{1,0:T(8,128)(2,1)} %hid_train.1, bf16[1008,512]{1,0:T(8,128)(2,1)} %head_ref.1, bf16[1008,512]{1,0:T(8,128)(2,1)} %head_train.1, s32[1,160]{1,0:T(1,128)} %bitcast.6, s32[1,160]{1,0:T(1,128)} %bitcast.7), custom_call_target="tpu_custom_call" | custom-call | tf_op jit(solution)/shard_map/fused/pallas_call | solution.py:641
  131.5 1.2 copy.12
  133.3 1.5 %copy.14 = f32[64,160]{1,0:T(8,128)} copy(f32[64,160]{1,0:T(8,128)} %get-tuple-element.14) | data formatting | bytes 81920
